TPU v7x, 256 devices: a whole 4x4x8 slice. The times are simulated.
256 devices in a mesh: gr: 16 (over z, core), gc: 16 (over x, y).
Axes of the slice: x: 4, y: 4, z: 8, core: 2. Of those that a mesh axis runs over, the one named last changes fastest.
Arguments:
- out_grad: bfloat16 [131072, 512], P(('gr', 'gc')), may hold values from -6 to 6
- preactivation_state: bfloat16 [131072, 512], P(('gr', 'gc')), may hold values from -6 to 6
- features: bfloat16 [131072, 512], P(('gc', 'gr')), may hold values from -24 to 24
- weight: bfloat16 [512, 512], replicated, may hold values from -0.25 to 0.25
- block_values: bfloat16 [16, 16, 152, 128, 128], P('gr', 'gc'), may hold values from -0.1875 to 0.1875
- block_rows: int32 [16, 16, 152], P('gr', 'gc'), may hold values from 0 to 63, as said below
- block_cols: int32 [16, 16, 152], P('gr', 'gc'), may hold values from 0 to 63, as said below
- block_counts: int32 [16, 16], P('gr', 'gc'), may hold values from 1 to 152, as said below
Outputs:
- input_grad: bfloat16 [131072, 512], P(('gc', 'gr'))
- weight_grad: float32 [512, 512], replicated
Inputs may be any that keep to these rules, and one draw needn't show every extreme that they name: `block_rows`: block row within a tile; some entry equals 63. `block_cols`: block column within a tile; some entry equals 63. `block_counts`: slots from this count on are unused; some tile uses all 152 slots.
All inputs are finite; a program needn't handle non-finite values.
Results may differ from a plain program's by a relative error of at most 0.014.
Values may be sent and summed in bfloat16 or wider, within the bound.
A program may use at most 128 MiB of HBM per device.

v0:
```python
import math

import jax
import jax.numpy as jnp
from jax import lax
from jax.sharding import PartitionSpec as P


def local(
    out_grad,
    preactivation_state,
    features,
    weight,
    block_values,
    block_rows,
    block_cols,
    block_counts,
):
    masked = jnp.where(preactivation_state > 0, out_grad, jnp.zeros_like(out_grad))
    tile_grads = lax.all_gather(masked, "gc", axis=0, tiled=True)
    block_size = block_values.shape[-1]
    feature_width = masked.shape[1]
    stacked = tile_grads.reshape(-1, block_size, feature_width)
    values_here = block_values[0, 0]
    rows_here = block_rows[0, 0]
    cols_here = block_cols[0, 0]
    count_here = block_counts[0, 0]
    capacity = values_here.shape[0]
    group_size = math.gcd(capacity, 16)
    node_rows = features.shape[0]
    col_count = node_rows * lax.axis_size("gr") // block_size

    def summing_group(current_index, value_partial_sum):
        offset = current_index * group_size
        current_values = lax.dynamic_slice_in_dim(values_here, offset, group_size, 0)
        rows_now = lax.dynamic_slice_in_dim(rows_here, offset, group_size, 0)
        cols_now = lax.dynamic_slice_in_dim(cols_here, offset, group_size, 0)
        selected_entries = stacked[rows_now]
        contribution = jnp.einsum(
            "yql,yqa->yla", current_values, selected_entries, preferred_element_type=jnp.float32
        )
        active = offset + jnp.arange(group_size) < count_here
        contribution = jnp.where(active[:, None, None], contribution, jnp.zeros_like(contribution))
        return value_partial_sum.at[cols_now].add(contribution)

    value_partial_sum = lax.fori_loop(
        0,
        capacity // group_size,
        summing_group,
        jnp.zeros((col_count, block_size, feature_width), jnp.float32),
    )
    value_partial_sum = value_partial_sum.reshape(-1, feature_width)
    column_total = lax.psum(value_partial_sum.astype(jnp.bfloat16), "gr").astype(jnp.float32)
    mine = lax.dynamic_slice_in_dim(column_total, lax.axis_index("gr") * node_rows, node_rows, 0)
    spread = mine.astype(jnp.bfloat16)
    input_grad = lax.dot_general(
        spread, weight, (((1,), (1,)), ((), ())), preferred_element_type=jnp.float32
    ).astype(jnp.bfloat16)
    weight_term = lax.dot_general(
        features, spread, (((0,), (0,)), ((), ())), preferred_element_type=jnp.float32
    )
    scale_factor = (node_rows * lax.axis_size("gr") * lax.axis_size("gc")) ** (-0.5)
    weight_grad = lax.psum(weight_term, ("gr", "gc")) * scale_factor
    return (input_grad, weight_grad)


def solution(mesh):
    in_specs = (
        P(("gr", "gc"), None),
        P(("gr", "gc"), None),
        P(("gc", "gr"), None),
        P(),
        P("gr", "gc", None, None, None),
        P("gr", "gc", None),
        P("gr", "gc", None),
        P("gr", "gc"),
    )
    out_specs = (P(("gc", "gr"), None), P())
    return jax.shard_map(local, mesh=mesh, in_specs=in_specs, out_specs=out_specs, check_vma=False)
```

profile of v0, /device:TPU:1, one launch (start us, length us, event | category | flops | bytes accessed | tf_op | source)
XLA Modules:
  0.0 736.2 jit_solution(15906717005274415228)
XLA Ops:
  9.4 7.7 %copy.10 = bf16[1,1,152,128,128]{3,4,2,1,0:T(8,128)(2,1)} copy(bf16[1,1,152,128,128]{4,3,2,1,0:T(8,128)(2,1)} %param.14) | data formatting | bytes 9961472 | tf_op args[4]
  17.1 73.6 %all-gather.2.cloned.1.call-done = bf16[8192,512]{1,0:T(8,128)(2,1)} async-done(((bf16[512,512]{1,0:T(8,128)(2,1)}), bf16[8192,512]{1,0:T(8,128)(2,1)}) %all-gather.2.cloned.1.call-update) | async-done | bytes 8388624 | tf_op jit(solution)/shard_map/all_gather | solution.py:20
  90.6 7.9 %broadcast_in_dim.38 = f32[64,128,512]{2,1,0:T(8,128)} broadcast(f32[]{:T(128)} %constant.51.clone.1), dimensions={} | broadcast | bytes 16777220 | tf_op jit(solution)/shard_map/broadcast_in_dim | solution.py:50
  98.5 224.6 %while.13 = (s32[]{:T(128)}, f32[64,128,512]{2,1,0:T(8,128)}, s32[152]{0:T(256)S(1)}, s32[]{:T(128)}, bf16[152,128,128]{1,2,0:T(8,128)(2,1)}, /*index=5*/s32[152...) while((s32[]{:T(128)}, f32[64,128,512]{2,1,0:T(8,128)}, ...), condition=%wide.region_2.3_spmd, body=%wide.region_0.2_spmd.sunk | while | flops 135267392 | bytes 11800995 | solution.py:46
  98.6 5.0 gather_fusion
  110.4 5.0 gather_fusion
  117.8 4.4 scatter_fusion
  122.3 5.0 gather_fusion
  134.1 5.0 gather_fusion
  145.9 5.0 gather_fusion
  157.7 5.0 gather_fusion
  169.5 5.0 gather_fusion
  181.4 5.0 gather_fusion
  193.2 5.0 gather_fusion
  200.6 4.4 scatter_fusion
  205.1 5.0 gather_fusion
  216.9 5.0 gather_fusion
  228.7 5.0 gather_fusion
  236.1 4.4 scatter_fusion
  240.6 5.0 gather_fusion
  252.4 5.0 gather_fusion
  259.7 4.4 scatter_fusion
  264.2 5.0 gather_fusion
  276.0 5.0 gather_fusion
  283.3 4.4 scatter_fusion
  287.8 5.0 gather_fusion
  299.6 5.0 gather_fusion
  307.0 4.5 scatter_fusion
  311.5 5.0 gather_fusion
  323.1 9.0 %convert_element_type.15 = bf16[64,128,512]{2,1,0:T(8,128)(2,1)} convert(f32[64,128,512]{2,1,0:T(8,128)} %get-tuple-element.126) | non-fusion elementwise | flops 4194304 | bytes 25165824 | tf_op jit(solution)/shard_map/convert_element_type | solution.py:53
  332.3 133.3 %all-reduce.3.cloned.1.call-done = bf16[8192,512]{1,0:T(8,128)(2,1)} async-done(((bf16[8192,512]{1,0:T(8,128)(2,1)}), bf16[8192,512]{1,0:T(8,128)(2,1)}) %all-reduce.3.cloned.1.call-update) | async-done | bytes 8388624 | tf_op jit(solution)/shard_map/psum | solution.py:53
  470.4 256.7 %all-reduce.5.cloned.1.call-done = f32[512,512]{0,1:T(8,128)} async-done(((f32[512,512]{0,1:T(8,128)}), f32[512,512]{0,1:T(8,128)}) %all-reduce.5.cloned.1.call-update) | async-done | bytes 1048592 | tf_op jit(solution)/shard_map/psum | solution.py:63
  (108 shorter events, 113.2 us)
Async XLA Ops:
  7.2 458.4 %copy-start = (bf16[512,512]{1,0:T(8,128)(2,1)S(1)}, bf16[512,512]{1,0:T(8,128)(2,1)}, u32[]{:S(2)}) copy-start(bf16[512,512]{1,0:T(8,128)(2,1)} %param.12) | copy-start | bytes 1572868
  7.2 83.4 %all-gather.2.cloned.1.call-start = ((), (), s32[]{:S(2)}) async-start(), calls=%async_computation | async-start | bytes 8912896 | tf_op jit(solution)/shard_map/all_gather | solution.py:20
  9.3 456.2 %all-reduce.3.cloned.1.call-start = ((), (), s32[]{:S(2)}) async-start(), calls=%async_computation.1 | async-start | bytes 16777216 | tf_op jit(solution)/shard_map/psum | solution.py:53
  90.6 7.9 %copy-start.2 = (s32[1,1,152]{2,1,0:T(1,128)S(1)}, s32[1,1,152]{2,1,0:T(1,128)}, u32[]{:S(2)}) copy-start(s32[1,1,152]{2,1,0:T(1,128)} %param.16) | copy-start | bytes 1828
  90.6 7.9 %copy-start.3 = (s32[1,1,152]{2,1,0:T(1,128)S(1)}, s32[1,1,152]{2,1,0:T(1,128)}, u32[]{:S(2)}) copy-start(s32[1,1,152]{2,1,0:T(1,128)} %param.15) | copy-start | bytes 1828
  332.2 135.9 %copy-start.1 = (bf16[512,512]{1,0:T(8,128)(2,1)S(1)}, bf16[512,512]{1,0:T(8,128)(2,1)}, u32[]{:S(2)}) copy-start(bf16[512,512]{1,0:T(8,128)(2,1)} %param.13) | copy-start | bytes 1572868
  332.2 394.9 %all-reduce.5.cloned.1.call-start = ((), (), s32[]{:S(2)}) async-start(), calls=%async_computation.2 | async-start | bytes 2097152 | tf_op jit(solution)/shard_map/psum | solution.py:63
Sparse Core Ops, SparseCore 0:
  11.0 79.5 all-gather.1
  332.3 133.1 all-reduce.2
  471.6 255.4 all-reduce.4
where the time goes:
time: 739 us; the launch traced here: 736 us
  waiting for transfers between devices  464 us (63%)
  local copies, waits for them, and re-layouts  111 us (15%)
  other arithmetic  110 us (15%)
  matrix products  37.8 us (5%)
  between operations  13.8 us (2%)
    psum x1, waiting for transfers between devices, local(): weight_grad = lax.psum(weight_term, ('gr', 'gc')) * scale_factor  257 us
    psum x1, waiting for transfers between devices, local(): lax.psum(value_partial_sum.astype(jnp.bfloat16), 'gr').astype(jnp.float32)  133 us
    gather x19, local copies, waits for them, and re-layouts, summing_group(): selected_entries = stacked[rows_now]  94.3 us
    scatter-add x19, other arithmetic, summing_group(): return value_partial_sum.at[cols_now].add(contribution)  83.2 us
    all_gather x1, waiting for transfers between devices, local(): tile_grads = lax.all_gather(masked, 'gc', axis=0, tiled=True)  73.6 us
    dot_general x19, matrix products, summing_group(): jnp.einsum('yql,yqa->yla', current_values, selected_entries, preferred_el...  33 us
  transfers between devices with their start and end apart: 3, of which 3 were waited for; matrix products, arithmetic and copies ran while one was open for 1% of the time, Pallas kernels for 0%

commit v1 on v0

v1 whole, which is shorter than its diff:
```python
import functools

import jax
import jax.numpy as jnp
from jax import lax
from jax.experimental import pallas as pl
from jax.experimental.pallas import tpu as pltpu
from jax.sharding import PartitionSpec as P

MESH = pl.DeviceIdType.MESH
B = 128
SLOTS = 152
CHUNKS = 4
UNROLL = 19
BF = jnp.bfloat16
F32 = jnp.float32


def kernel(
    packed, last, og_h, pre_h, feat_h, w_h, vals_h,
    ig_o, wg_o,
    g0, g1, g2, g3, og, pre, feat, w, vals, prods, part, sib, zs, zr, spread, term, tsend, trecv,
    psend, precv, zx, wg,
    local_sem, g_send, g_recv, e_send, e_recv, z_send, z_recv, t_send, t_recv, p_send, p_recv,
    x_send, x_recv, q_send, q_recv, c_send, c_recv,
):
    gathered = (g0, g1, g2, g3)
    gr, gc = lax.axis_index("gr"), lax.axis_index("gc")
    z, core = gr // 2, gr % 2
    x, y = gc // 4, gc % 4
    sibling = {"gr": z * 2 + (1 - core), "gc": gc}

    def z_peer(d):
        return {"gr": ((z + d) % 8) * 2 + core, "gc": gc}

    def plane_peer(d):
        return {"gr": gr, "gc": (gc + d) % 16}

    def x_peer(d):
        return {"gr": gr, "gc": ((x + d + 4) % 4) * 4 + y}

    def y_peer(d):
        return {"gr": gr, "gc": x * 4 + (y + d + 4) % 4}

    loads = [
        pltpu.make_async_copy(og_h, og, local_sem.at[0]),
        pltpu.make_async_copy(pre_h, pre, local_sem.at[1]),
        pltpu.make_async_copy(vals_h, vals, local_sem.at[2]),
        pltpu.make_async_copy(feat_h, feat, local_sem.at[3]),
        pltpu.make_async_copy(w_h, w, local_sem.at[4]),
    ]
    for load in loads:
        load.start()

    barrier = pltpu.get_barrier_semaphore()
    pl.semaphore_signal(barrier, inc=1, device_id=sibling, device_id_type=MESH)

    def greet_z(d, _):
        pl.semaphore_signal(barrier, inc=1, device_id=z_peer(d), device_id_type=MESH)
        return 0

    def greet_plane(d, _):
        pl.semaphore_signal(barrier, inc=1, device_id=plane_peer(d), device_id_type=MESH)
        return 0

    lax.fori_loop(1, 8, greet_z, 0)
    lax.fori_loop(1, 16, greet_plane, 0)

    ring = (x, y)
    cross = (y, x)
    near = (x_peer, y_peer)
    far = (y_peer, x_peer)

    def unit(h, p, q):
        return h * 32 + p * 8 + q * 2

    loads[0].wait()
    loads[1].wait()
    for k in range(CHUNKS):
        for b in range(4):
            rows, cols = pl.ds(b * B, B), pl.ds(k * B, B)
            block = og[rows, cols]
            block = jnp.where(pre[rows, cols].astype(F32) > 0, block.astype(F32), 0.0)
            h = b // 2
            gathered[k][unit(h, cross[h], ring[h]) + b % 2] = block.T.astype(BF)
    prods[SLOTS] = jnp.zeros((B, B), BF)
    pl.semaphore_wait(barrier, 23)

    sent = []
    pending = {}

    def send(key, src, dst, send_sem, recv_sem, device):
        copy = pltpu.make_async_remote_copy(
            src_ref=src, dst_ref=dst, send_sem=send_sem, recv_sem=recv_sem, device_id=device, device_id_type=MESH
        )
        copy.start()
        sent.append(copy)
        pending[key] = copy

    def arrived(key):
        pending.pop(key).wait_recv()

    def gather_copy(stage, k, h, d, at, size, device):
        n = ((k * 5 + stage) * 2 + h) * 2 + (d + 1) // 2
        where = gathered[k].at[pl.ds(at, size)]
        send(("g", stage, k, h, d), where, where, g_send.at[n], g_recv.at[n], device)

    def first_ring(k):
        for h in range(2):
            for d in (1, -1):
                gather_copy(0, k, h, d, unit(h, cross[h], ring[h]), 2, near[h](d))

    def first_forward(k):
        for h in range(2):
            for d in (1, -1):
                arrived(("g", 0, k, h, d))
                came = (ring[h] - d + 4) % 4
                gather_copy(1, k, h, d, unit(h, cross[h], came) + (0 if d == 1 else 1), 1, near[h](d))

    def second_ring(k):
        for h in range(2):
            for d in (1, -1):
                arrived(("g", 1, k, h, d))
            for part_no in range(2):
                for d in (1, -1):
                    which = part_no if d == 1 else 1 - part_no
                    gather_copy(2 + part_no, k, h, d, unit(h, cross[h], 0) + 4 * which, 4, far[h](d))

    def second_forward(k):
        for h in range(2):
            for d in (1, -1):
                arrived(("g", 2, k, h, d))
                came = (cross[h] - d + 4) % 4
                gather_copy(4, k, h, d, unit(h, came, 0) + (0 if d == 1 else 4), 4, far[h](d))

    def gather_end(k):
        for stage in (3, 4):
            for h in range(2):
                for d in (1, -1):
                    arrived(("g", stage, k, h, d))

    order = (4, 3, 5, 2, 6, 1, 7, 0)

    def multiply(k):
        source = gathered[k]

        def some(t, total):
            for u in range(UNROLL):
                s = t * UNROLL + u
                word = packed[s]
                term_now = jnp.dot(source[(word >> 8) & 255], vals[word & 255], preferred_element_type=F32)
                total = jnp.where((word >> 16) != 0, term_now, total + term_now)
                prods[s] = total.astype(BF)
            return total

        lax.fori_loop(0, SLOTS // UNROLL, some, jnp.zeros((B, B), F32))
        for d in order:
            zp = (z + d) % 8

            def place(j, _):
                part[k, zp * 8 + j] = prods[last[zp * 8 + j]]
                return 0

            lax.fori_loop(0, 8, place, 0, unroll=True)
            n = k * 8 + d
            send(
                ("e", k, d), part.at[k, pl.ds(zp * 8 + (1 - core) * 4, 4)], sib.at[k, pl.ds(zp * 4, 4)],
                e_send.at[n], e_recv.at[n], sibling,
            )

    def own(k, zp, b):
        return part[k, zp * 8 + core * 4 + b].astype(F32) + sib[k, zp * 4 + b].astype(F32)

    def z_copy(k, side, t, low, size):
        n = (k * 2 + side) * 4 + t - 1
        send(
            ("z", k, side, t), zs.at[n, pl.ds(low, size)], zr.at[n, pl.ds(low, size)],
            z_send.at[n], z_recv.at[n], z_peer(7 if side == 0 else 1),
        )

    def z_step(k, t):
        if t == 4:
            arrived(("e", k, 4))
            zp = (z + 4) % 8
            for side in range(2):
                n = (k * 2 + side) * 4 + 3
                for b in (2 * side, 2 * side + 1):
                    zs[n, b] = own(k, zp, b).astype(BF)
                z_copy(k, side, 4, 2 * side, 2)
            return
        for side in range(2):
            d = 8 - t if side == 0 else t
            zp = (z + d) % 8
            n = (k * 2 + side) * 4 + t - 1
            arrived(("e", k, d))
            arrived(("z", k, side, t + 1))
            for b in range(4):
                value = own(k, zp, b)
                if t < 3 or b // 2 == side:
                    value = value + zr[n + 1, b].astype(F32)
                zs[n, b] = value.astype(BF)
            z_copy(k, side, t, 0, 4)

    def z_end(k):
        arrived(("e", k, 0))
        arrived(("z", k, 0, 1))
        arrived(("z", k, 1, 1))
        for b in range(4):
            total = own(k, z, b) + zr[k * 8, b].astype(F32) + zr[k * 8 + 4, b].astype(F32)
            spread[k * 4 + b] = total.astype(BF)

    def weight_term(k):
        total = jnp.dot(spread[k * 4], feat[pl.ds(0, B), :], preferred_element_type=F32)
        for b in range(1, 4):
            total = total + jnp.dot(spread[k * 4 + b], feat[pl.ds(b * B, B), :], preferred_element_type=F32)
        term[k] = total
        tsend[k] = term[k, pl.ds((1 - core) * 64, 64), :].astype(BF)
        send(("t", k), tsend.at[k], trecv.at[k], t_send.at[k], t_recv.at[k], sibling)

    def plane_scatter(k):
        arrived(("t", k))
        for a in range(4):
            for b in range(4):
                lanes = pl.ds(b * B, B)
                mine = term[k, pl.ds(core * 64 + a * 16, 16), lanes]
                psend[k, a * 4 + b] = (mine + trecv[k, pl.ds(a * 16, 16), lanes].astype(F32)).astype(BF)
        for o in range(1, 16):
            n = k * 15 + o - 1
            to = plane_peer(o)
            send(("p", k, o), psend.at[k, to["gc"]], precv.at[k, o - 1], p_send.at[n], p_recv.at[n], to)

    def z_exchange(k):
        total = psend[k, gc].astype(F32)
        for o in range(1, 16):
            arrived(("p", k, o))
            total = total + precv[k, o - 1].astype(F32)
        zx[k, z] = total.astype(BF)
        for o in range(1, 8):
            n = k * 7 + o - 1
            send(("x", k, o), zx.at[k, z], zx.at[k, z], x_send.at[n], x_recv.at[n], z_peer(o))

    def plane_gather(k):
        for o in range(1, 8):
            arrived(("x", k, o))
        total = zx[k, 0].astype(F32)
        for a in range(1, 8):
            total = total + zx[k, a].astype(F32)
        wg[k, core, gc] = total.astype(BF)
        for o in range(1, 16):
            n = k * 15 + o - 1
            send(("q", k, o), wg.at[k, core, gc], wg.at[k, core, gc], q_send.at[n], q_recv.at[n], plane_peer(o))

    def core_gather(k):
        for o in range(1, 16):
            arrived(("q", k, o))
        send(("c", k), wg.at[k, core], wg.at[k, core], c_send.at[k], c_recv.at[k], sibling)

    def weight_out(k):
        arrived(("c", k))
        for c in range(2):
            for a in range(4):
                for b in range(4):
                    wg_o[pl.ds(k * B + c * 64 + a * 16, 16), pl.ds(b * B, B)] = wg[k, c, a * 4 + b]

    def input_rows(b):
        total = jnp.zeros((B, 512), F32)
        for k in range(CHUNKS):
            total = total + lax.dot_general(
                spread[k * 4 + b].T, w[:, pl.ds(k * B, B)], (((1,), (1,)), ((), ())), preferred_element_type=F32
            )
        ig_o[pl.ds(b * B, B), :] = total.astype(BF)

    first_ring(0)
    first_ring(1)
    first_forward(0)
    second_ring(0)
    first_forward(1)
    first_ring(2)
    second_forward(0)
    second_ring(1)
    first_forward(2)
    first_ring(3)
    for load in loads[2:]:
        load.wait()
    gather_end(0)

    multiply(0)
    second_forward(1)
    second_ring(2)
    first_forward(3)
    z_step(0, 4)
    z_step(0, 3)
    z_step(0, 2)
    gather_end(1)

    multiply(1)
    z_step(0, 1)
    second_forward(2)
    second_ring(3)
    z_end(0)
    weight_term(0)
    z_step(1, 4)
    plane_scatter(0)
    z_step(1, 3)
    z_exchange(0)
    z_step(1, 2)
    plane_gather(0)
    gather_end(2)

    multiply(2)
    z_step(1, 1)
    second_forward(3)
    core_gather(0)
    z_end(1)
    weight_term(1)
    z_step(2, 4)
    plane_scatter(1)
    z_step(2, 3)
    z_exchange(1)
    z_step(2, 2)
    plane_gather(1)
    gather_end(3)

    multiply(3)
    z_step(2, 1)
    core_gather(1)
    z_end(2)
    weight_term(2)
    z_step(3, 4)
    plane_scatter(2)
    z_step(3, 3)
    z_exchange(2)
    z_step(3, 2)
    plane_gather(2)
    z_step(3, 1)
    weight_out(0)
    weight_out(1)
    core_gather(2)
    z_end(3)
    weight_term(3)
    plane_scatter(3)
    input_rows(0)
    input_rows(1)
    z_exchange(3)
    input_rows(2)
    plane_gather(3)
    input_rows(3)
    weight_out(2)
    core_gather(3)
    for copy in sent:
        copy.wait_send()
    weight_out(3)


def local(out_grad, state, features, weight, block_values, block_rows, block_cols, block_counts):
    values, rows, cols, count = block_values[0, 0], block_rows[0, 0], block_cols[0, 0], block_counts[0, 0]
    slot = jnp.arange(SLOTS, dtype=jnp.int32)
    key = jnp.where(slot < count, cols, 64)
    before = (key[None, :] < key[:, None]) | ((key[None, :] == key[:, None]) & (slot[None, :] < slot[:, None]))
    rank = jnp.sum(before.astype(jnp.int32), axis=1)
    first = jnp.sum(((key[None, :] == key[:, None]) & (slot[None, :] < slot[:, None])).astype(jnp.int32), axis=1) == 0
    device, b = rows // 4, rows % 4
    a0, a1 = device // 4, device % 4
    place = jnp.where(b < 2, a1 * 8 + a0 * 2 + b, 32 + a0 * 8 + a1 * 2 + b - 2)
    word = slot | (place << 8) | (first.astype(jnp.int32) << 16)
    packed = jnp.sum(jnp.where(rank[None, :] == slot[:, None], word[None, :], 0), axis=1)
    column = jnp.arange(64, dtype=jnp.int32)
    upto = jnp.sum((key[None, :] <= column[:, None]).astype(jnp.int32), axis=1)
    here = jnp.sum((key[None, :] == column[:, None]).astype(jnp.int32), axis=1)
    last = jnp.where(here > 0, upto - 1, SLOTS)

    anywhere = pl.BlockSpec(memory_space=pl.ANY)
    dma = pltpu.SemaphoreType.DMA
    grid = (512, 512)
    ig, wg = pl.pallas_call(
        kernel,
        out_shape=(jax.ShapeDtypeStruct(grid, BF), jax.ShapeDtypeStruct(grid, BF)),
        in_specs=[pl.BlockSpec(memory_space=pltpu.SMEM)] * 2 + [anywhere] * 5,
        out_specs=(pl.BlockSpec(memory_space=pltpu.VMEM), pl.BlockSpec(memory_space=pltpu.VMEM)),
        scratch_shapes=[pltpu.VMEM((64, B, B), BF)] * 4
        + [pltpu.VMEM(grid, BF)] * 4
        + [
            pltpu.VMEM((SLOTS, B, B), BF),
            pltpu.VMEM((SLOTS + 1, B, B), BF),
            pltpu.VMEM((CHUNKS, 64, B, B), BF),
            pltpu.VMEM((CHUNKS, 32, B, B), BF),
            pltpu.VMEM((CHUNKS * 8, 4, B, B), BF),
            pltpu.VMEM((CHUNKS * 8, 4, B, B), BF),
            pltpu.VMEM((CHUNKS * 4, B, B), BF),
            pltpu.VMEM((CHUNKS, B, 512), F32),
            pltpu.VMEM((CHUNKS, 64, 512), BF),
            pltpu.VMEM((CHUNKS, 64, 512), BF),
            pltpu.VMEM((CHUNKS, 16, 16, B), BF),
            pltpu.VMEM((CHUNKS, 15, 16, B), BF),
            pltpu.VMEM((CHUNKS, 8, 16, B), BF),
            pltpu.VMEM((CHUNKS, 2, 16, 16, B), BF),
            dma((5,)),
            dma((CHUNKS * 20,)),
            dma((CHUNKS * 20,)),
            dma((CHUNKS * 8,)),
            dma((CHUNKS * 8,)),
            dma((CHUNKS * 8,)),
            dma((CHUNKS * 8,)),
            dma((CHUNKS,)),
            dma((CHUNKS,)),
            dma((CHUNKS * 15,)),
            dma((CHUNKS * 15,)),
            dma((CHUNKS * 7,)),
            dma((CHUNKS * 7,)),
            dma((CHUNKS * 15,)),
            dma((CHUNKS * 15,)),
            dma((CHUNKS,)),
            dma((CHUNKS,)),
        ],
        compiler_params=pltpu.CompilerParams(
            collective_id=0, has_side_effects=True, vmem_limit_bytes=56 * 1024 * 1024
        ),
        name="graph_backward",
    )(packed, last, out_grad, state, features, weight, values)
    nodes = 512 * lax.axis_size("gr") * lax.axis_size("gc")
    return ig, wg.T.astype(F32) * nodes ** (-0.5)


def solution(mesh):
    in_specs = (
        P(("gr", "gc"), None),
        P(("gr", "gc"), None),
        P(("gc", "gr"), None),
        P(),
        P("gr", "gc", None, None, None),
        P("gr", "gc", None),
        P("gr", "gc", None),
        P("gr", "gc"),
    )
    out_specs = (P(("gc", "gr"), None), P())
    return jax.shard_map(local, mesh=mesh, in_specs=in_specs, out_specs=out_specs, check_vma=False)
```

time: 739 us -> 148 us (0.20)
  waiting for transfers between devices: 464 us -> 0 us
  Pallas kernels: 0 us -> 139 us
  local copies, waits for them, and re-layouts: 111 us -> 3.18 us
  other arithmetic: 110 us -> 4.12 us
  matrix products: 37.8 us -> 0 us
  between operations: 13.8 us -> 1.3 us
    psum x2 -> x0, waiting for transfers between devices: 390 us -> none  [the longest x1 257 us: local(): weight_grad = lax.psum(weight_term, ('gr', 'gc')) * scale_factor]
    pallas_call x0 -> x1, Pallas kernels: none -> 139 us  [local(): pl.pallas_call(kernel, out_shape=(jax.ShapeDtypeStruct(grid, BF), jax.Sha...]
    gather x19 -> x0, local copies, waits for them, and re-layouts: 94.3 us -> none  [summing_group(): selected_entries = stacked[rows_now]]
    scatter-add x19 -> x0, other arithmetic: 83.2 us -> none  [summing_group(): return value_partial_sum.at[cols_now].add(contribution)]
    all_gather x1 -> x0, waiting for transfers between devices: 73.6 us -> none  [local(): tile_grads = lax.all_gather(masked, 'gc', axis=0, tiled=True)]
    dot_general x21 -> x0, matrix products: 37.8 us -> none  [the longest x19 33 us: summing_group(): jnp.einsum('yql,yqa->yla', current_values, selected_entries, preferred_el...]
    lt x19 -> x0, other arithmetic: 12.3 us -> none  [summing_group(): active = offset + jnp.arange(group_size) < count_here]
    convert_element_type x1 -> x0, other arithmetic: 9.03 us -> none  [local(): value_partial_sum.astype(jnp.bfloat16)]
  transfers between devices with their start and end apart: 3 -> 0, of which waited for: 3 -> 0; matrix products, arithmetic and copies ran while one was open for 1% -> 0% of each run, Pallas kernels for 0% -> 0%
where the time goes in v1:
time: 148 us; the launch traced here: 147 us
  Pallas kernels  139 us (94%)
  other arithmetic  4.12 us (3%)
  local copies, waits for them, and re-layouts  3.18 us (2%)
    pallas_call x1, Pallas kernels, local(): pl.pallas_call(kernel, out_shape=(jax.ShapeDtypeStruct(grid, BF), jax.Sha...  139 us
    unnamed x2, local copies, waits for them, and re-layouts  3.18 us

profile of v1, /device:TPU:1, one launch (start us, length us, event | category | flops | bytes accessed | tf_op | source)
XLA Modules:
  0.0 147.4 jit_solution(9887628193302452745)
XLA Ops:
  1.3 0.7 compare_select_fusion.2
  2.0 0.1 convert_reduce_fusion.2
  2.1 0.5 compare_select_fusion.last
  2.6 0.2 convert_reduce_fusion.1
  2.8 0.7 fusion.3
  3.5 0.7 select_reduce_fusion.packed
  4.2 138.8 %graph_backward.1 = (bf16[512,512]{1,0:T(8,128)(2,1)}, bf16[512,512]{1,0:T(8,128)(2,1)}) custom-call(s32[152]{0:T(256)} %select_reduce_fusion.packed, s32[64]{0:T(128)} %compare_select_fusion.last, bf16[512,512]{1,0:T(8,128)(2,1)} %og_h.1, bf16[512,512]{1,0:T(8,128)(2,1)} %pre_h.1, bf16[512,512]{1,0:T(8,128)(2,1)} %feat_h.1, bf16[512,512]{1,0:T(8,128)(2,1)} %w_h.1, ...), custom_call_target="tpu_custom_call" | custom-call | tf_op jit(solution)/shard_map/graph_backward/pallas_call | solution.py:375
  143.0 1.2 multiply_bitcast_fusion
  144.2 1.3 copy.11
  145.5 1.9 %copy.14 = bf16[512,512]{1,0:T(8,128)(2,1)} copy(bf16[512,512]{1,0:T(8,128)(2,1)} %get-tuple-element.16) | data formatting | bytes 1048576

commit v2 on v1

v2 whole, which is shorter than its diff:
```python
import functools

import jax
import jax.numpy as jnp
from jax import lax
from jax.experimental import pallas as pl
from jax.experimental.pallas import tpu as pltpu
from jax.sharding import PartitionSpec as P

MESH = pl.DeviceIdType.MESH
B = 128
SLOTS = 152
CUTS = ((0, 64), (64, 64), (128, 128), (256, 128), (384, 64), (448, 64))
CHUNKS = len(CUTS)
UNITS = 4
UNROLL = 19
BF = jnp.bfloat16
F32 = jnp.float32


GROUPS = ((4,), (3, 5), (2, 6), (1, 7), (0,))


def plan():
    tasks = {}

    def task(name, args, after=(), needs=(), sends=(), cost=0.1, rank=0.0):
        tasks[name, args] = (tuple(after), tuple(needs), tuple(sends), cost, rank)

    chip, core = 2.4, 0.9
    task("loads", (), cost=0.1, rank=0)
    for k, (at, size) in enumerate(CUTS):
        unit = size / 2
        task("ring1", (k,), [("ring1", (k - 1,))] if k else [], (), [(("r1", k), "xy", unit, chip)], rank=-9)
        task("pass1", (k,), [], [("r1", k)], [(("f1", k), "xy", unit / 2, chip)], rank=-8)
        before = max(0, k - 1 - (size == 64))
        gate = [("pass2", (before,))] if k > 1 else []
        task(
            "ring2", (k,), gate + ([("ring2", (k - 1,))] if k else []), [("f1", k)],
            [(("a", k), "xy", unit * 2, chip), (("b", k), "xy", unit * 2, chip)], rank=-7,
        )
        task("pass2", (k,), [], [("a", k)], [(("f2", k), "xy", unit * 2, chip)], rank=-8)
        load = 0.5 + size / 128
        follow = [("place", (k - 1, GROUPS[-1]))] if k else [("loads", ())]
        task("mult", (k, 0), follow, [("b", k), ("f2", k)], cost=load, rank=k)
        task("mult", (k, 1), [("mult", (k, 0))], cost=load, rank=k)
        for i, group in enumerate(GROUPS):
            task(
                "place", (k, group), [("place", (k, GROUPS[i - 1])) if i else ("mult", (k, 1))], (),
                [(("e", k, d), "core", size, core) for d in group], 0.08 * len(group), k - 0.5,
            )
        for chain in range(2):
            for t in range(4 - chain, 0, -1):
                needs = [("e", k, d) for d in {t, 8 - t}]
                if t < 4 - chain:
                    needs.append(("z", k, chain, t + 1))
                task("z", (k, chain, t), (), needs, [(("z", k, chain, t), "z", size / 2, chip)], 0.2, -6 + k / 10)
        task("zend", (k,), (), [("e", k, 0), ("z", k, 0, 1), ("z", k, 1, 1)], cost=0.25, rank=-5 + k / 10)
    for u in range(UNITS):
        ends = [("zend", (k,)) for k, (at, _) in enumerate(CUTS) if at // B == u]
        task("term", (u,), ends, (), [(("t", u), "core", 64, core)], 0.7, u - 1)
        task("scatter", (u,), (), [("t", u)], [(("p", u), "xy", 32, 4.5)], 0.5, u - 1)
        task("zsum", (u,), (), [("p", u)], [(("x", u), "z", 32, 4.5)], 0.4, u - 1)
        task("gather", (u,), (), [("x", u)], [(("q", u), "xy", 32, 4.5)], 0.5, u - 1)
        task("core", (u,), (), [("q", u)], [(("c", u), "core", 64, core)], 0.2, u - 1)
        task("out", (u,), (), [("c", u)], cost=0.4, rank=u + 1)
    for b in range(4):
        task("rows", (b,), [("zend", (CHUNKS - 1,)), ("scatter", (UNITS - 1,))], cost=0.6, rank=20)
    for i, stage in enumerate(("zend", "zsum", "gather")):
        stage_args = (CHUNKS - 2,) if stage == "zend" else (UNITS - 1,)
        task("drain", (i,), [(stage, stage_args)], cost=1.0, rank=30)

    now, free, come, done, order = 0.0, {"xy": 0.0, "z": 0.0, "core": 0.0}, {}, set(), []
    rate = {"xy": 48.0, "z": 48.0, "core": 600.0}
    while tasks:
        best = None
        for key, (after, needs, _, cost, rank) in tasks.items():
            if all(a in done for a in after) and all(n in come for n in needs):
                ready = max([now] + [come[n] for n in needs])
                score = (ready, rank)
                if best is None or score < best[0]:
                    best = (score, key)
        (now, _), key = best
        _, _, sends, cost, _ = tasks.pop(key)
        now += cost
        for message, link, kib, latency in sends:
            free[link] = max(free[link], now) + kib / rate[link]
            come[message] = free[link] + latency
        done.add(key)
        order.append(key)
    return order


def kernel(
    packed, last, og_h, pre_h, feat_h, w_h, vals_h,
    ig_o, wg_o,
    g0, g1, g2, g3, g4, g5, og, pre, feat, w, vals, prods, carry, part, sib, zs, zr, spread, term, tsend, trecv,
    psend, precv, zx, wg,
    local_sem, g_send, g_recv, e_send, e_recv, z_send, z_recv, t_send, t_recv, p_send, p_recv,
    x_send, x_recv, q_send, q_recv, c_send, c_recv,
):
    gathered = (g0, g1, g2, g3, g4, g5)
    gr, gc = lax.axis_index("gr"), lax.axis_index("gc")
    z, core = gr // 2, gr % 2
    x, y = gc // 4, gc % 4
    sibling = {"gr": z * 2 + (1 - core), "gc": gc}

    def z_peer(d):
        return {"gr": ((z + d) % 8) * 2 + core, "gc": gc}

    def plane_peer(d):
        return {"gr": gr, "gc": (gc + d) % 16}

    def x_peer(d):
        return {"gr": gr, "gc": ((x + d + 4) % 4) * 4 + y}

    def y_peer(d):
        return {"gr": gr, "gc": x * 4 + (y + d + 4) % 4}

    loads = [
        pltpu.make_async_copy(og_h, og, local_sem.at[0]),
        pltpu.make_async_copy(pre_h, pre, local_sem.at[1]),
        pltpu.make_async_copy(vals_h, vals, local_sem.at[2]),
        pltpu.make_async_copy(feat_h, feat, local_sem.at[3]),
        pltpu.make_async_copy(w_h, w, local_sem.at[4]),
    ]
    for load in loads:
        load.start()

    barrier = pltpu.get_barrier_semaphore()
    pl.semaphore_signal(barrier, inc=1, device_id=sibling, device_id_type=MESH)

    def greet_z(d, _):
        pl.semaphore_signal(barrier, inc=1, device_id=z_peer(d), device_id_type=MESH)
        return 0

    def greet_plane(d, _):
        pl.semaphore_signal(barrier, inc=1, device_id=plane_peer(d), device_id_type=MESH)
        return 0

    lax.fori_loop(1, 8, greet_z, 0)
    lax.fori_loop(1, 16, greet_plane, 0)

    ring = (x, y)
    cross = (y, x)
    near = (x_peer, y_peer)
    far = (y_peer, x_peer)

    def unit(h, p, q):
        return h * 32 + p * 8 + q * 2

    loads[0].wait()
    loads[1].wait()
    for k in range(UNITS):
        for b in range(4):
            rows, cols = pl.ds(b * B, B), pl.ds(k * B, B)
            block = og[rows, cols]
            block = jnp.where(pre[rows, cols].astype(F32) > 0, block.astype(F32), 0.0).T.astype(BF)
            h = b // 2
            for n, (at, size) in enumerate(CUTS):
                if at // B == k:
                    gathered[n][unit(h, cross[h], ring[h]) + b % 2] = block[at % B : at % B + size]
    prods[SLOTS] = jnp.zeros((B, B), BF)
    pl.semaphore_wait(barrier, 23)

    sent = []
    pending = {}

    def send(key, src, dst, send_sem, recv_sem, device):
        copy = pltpu.make_async_remote_copy(
            src_ref=src, dst_ref=dst, send_sem=send_sem, recv_sem=recv_sem, device_id=device, device_id_type=MESH
        )
        copy.start()
        sent.append(copy)
        pending[key] = copy

    def arrived(key):
        pending.pop(key).wait_recv()

    def gather_copy(stage, k, h, d, at, size, device):
        n = ((k * 5 + stage) * 2 + h) * 2 + (d + 1) // 2
        where = gathered[k].at[pl.ds(at, size)]
        send(("g", stage, k, h, d), where, where, g_send.at[n], g_recv.at[n], device)

    def first_ring(k):
        for h in range(2):
            for d in (1, -1):
                gather_copy(0, k, h, d, unit(h, cross[h], ring[h]), 2, near[h](d))

    def first_forward(k):
        for h in range(2):
            for d in (1, -1):
                arrived(("g", 0, k, h, d))
                came = (ring[h] - d + 4) % 4
                gather_copy(1, k, h, d, unit(h, cross[h], came) + (0 if d == 1 else 1), 1, near[h](d))

    def second_ring(k):
        for h in range(2):
            for d in (1, -1):
                arrived(("g", 1, k, h, d))
        for part_no in range(2):
            for h in range(2):
                for d in (1, -1):
                    which = part_no if d == 1 else 1 - part_no
                    gather_copy(2 + part_no, k, h, d, unit(h, cross[h], 0) + 4 * which, 4, far[h](d))

    def second_forward(k):
        for h in range(2):
            for d in (1, -1):
                arrived(("g", 2, k, h, d))
                came = (cross[h] - d + 4) % 4
                gather_copy(4, k, h, d, unit(h, came, 0) + (0 if d == 1 else 4), 4, far[h](d))

    def multiply(k, half):
        at, size = CUTS[k]
        source = gathered[k]
        if half == 0:
            for stage in (3, 4):
                for h in range(2):
                    for d in (1, -1):
                        arrived(("g", stage, k, h, d))

        def some(t, total):
            for u in range(UNROLL):
                s = (half * 4 + t) * UNROLL + u
                word = packed[s]
                term_now = jnp.dot(source[(word >> 8) & 255], vals[word & 255], preferred_element_type=F32)
                total = jnp.where((word >> 16) != 0, term_now, total + term_now)
                prods[s, pl.ds(0, size)] = total.astype(BF)
            return total

        begin = jnp.zeros((size, B), F32) if half == 0 else carry[pl.ds(0, size), :]
        total = lax.fori_loop(0, SLOTS // UNROLL // 2, some, begin)
        if half == 0:
            carry[pl.ds(0, size), :] = total

    def place(k, group):
        at, size = CUTS[k]
        for d in group:
            zp = (z + d) % 8

            def one(j, _):
                part[zp * 8 + j, pl.ds(at, size)] = prods[last[zp * 8 + j], pl.ds(0, size)]
                return 0

            lax.fori_loop(0, 8, one, 0, unroll=True)
            n = k * 8 + d
            send(
                ("e", k, d),
                part.at[pl.ds(zp * 8 + (1 - core) * 4, 4), pl.ds(at, size)],
                sib.at[pl.ds(zp * 4, 4), pl.ds(at, size)],
                e_send.at[n], e_recv.at[n], sibling,
            )

    exchanged = set()

    def own(k, d, b):
        if (k, d) not in exchanged:
            exchanged.add((k, d))
            arrived(("e", k, d))
        zp = (z + d) % 8
        cut = pl.ds(*CUTS[k])
        return part[zp * 8 + core * 4 + b, cut].astype(F32) + sib[zp * 4 + b, cut].astype(F32)

    def z_step(k, chain, t):
        cut = pl.ds(*CUTS[k])
        for side in range(2):
            h = side if chain == 0 else 1 - side
            d = 8 - t if side == 0 else t
            n = side * 4 + t - 1
            fresh = t == 4 - chain
            if not fresh:
                arrived(("z", k, chain, side, t + 1))
            for b in (2 * h, 2 * h + 1):
                value = own(k, d, b)
                if not fresh:
                    value = value + zr[n + 1, b, cut].astype(F32)
                zs[n, b, cut] = value.astype(BF)
            m = (k * 2 + side) * 7 + (t + 2 if chain == 0 else t - 1)
            blocks = pl.ds(2 * h, 2)
            send(
                ("z", k, chain, side, t), zs.at[n, blocks, cut], zr.at[n, blocks, cut],
                z_send.at[m], z_recv.at[m], z_peer(7 if side == 0 else 1),
            )

    def z_end(k):
        cut = pl.ds(*CUTS[k])
        for chain in range(2):
            for side in range(2):
                arrived(("z", k, chain, side, 1))
        for b in range(4):
            total = own(k, 0, b) + zr[0, b, cut].astype(F32) + zr[4, b, cut].astype(F32)
            spread[b, cut] = total.astype(BF)

    def weight_term(k):
        total = jnp.dot(spread[0, pl.ds(k * B, B)], feat[pl.ds(0, B), :], preferred_element_type=F32)
        for b in range(1, 4):
            rows = spread[b, pl.ds(k * B, B)]
            total = total + jnp.dot(rows, feat[pl.ds(b * B, B), :], preferred_element_type=F32)
        term[k] = total
        tsend[k] = term[k, pl.ds((1 - core) * 64, 64), :].astype(BF)
        send(("t", k), tsend.at[k], trecv.at[k], t_send.at[k], t_recv.at[k], sibling)

    def plane_scatter(k):
        arrived(("t", k))
        for a in range(4):
            for b in range(4):
                lanes = pl.ds(b * B, B)
                mine = term[k, pl.ds(core * 64 + a * 16, 16), lanes]
                psend[k, a * 4 + b] = (mine + trecv[k, pl.ds(a * 16, 16), lanes].astype(F32)).astype(BF)
        for o in range(1, 16):
            n = k * 15 + o - 1
            to = plane_peer(o)
            send(("p", k, o), psend.at[k, to["gc"]], precv.at[k, o - 1], p_send.at[n], p_recv.at[n], to)

    def z_exchange(k):
        total = psend[k, gc].astype(F32)
        for o in range(1, 16):
            arrived(("p", k, o))
            total = total + precv[k, o - 1].astype(F32)
        zx[k, z] = total.astype(BF)
        for o in range(1, 8):
            n = k * 7 + o - 1
            send(("x", k, o), zx.at[k, z], zx.at[k, z], x_send.at[n], x_recv.at[n], z_peer(o))

    def plane_gather(k):
        for o in range(1, 8):
            arrived(("x", k, o))
        total = zx[k, 0].astype(F32)
        for a in range(1, 8):
            total = total + zx[k, a].astype(F32)
        wg[k, core, gc] = total.astype(BF)
        for o in range(1, 16):
            n = k * 15 + o - 1
            send(("q", k, o), wg.at[k, core, gc], wg.at[k, core, gc], q_send.at[n], q_recv.at[n], plane_peer(o))

    def core_gather(k):
        for o in range(1, 16):
            arrived(("q", k, o))
        send(("c", k), wg.at[k, core], wg.at[k, core], c_send.at[k], c_recv.at[k], sibling)

    def weight_out(k):
        arrived(("c", k))
        for b in range(4):
            rows = [wg[k, c, a * 4 + b] for c in range(2) for a in range(4)]
            whole = jnp.concatenate(rows, axis=0).astype(F32)
            wg_o[pl.ds(b * B, B), pl.ds(k * B, B)] = whole.T.astype(BF)

    def input_rows(b):
        total = lax.dot_general(spread[b].T, w[...], (((1,), (1,)), ((), ())), preferred_element_type=F32)
        ig_o[pl.ds(b * B, B), :] = total.astype(BF)

    def drain(_):
        for copy in sent:
            copy.wait_send()
        sent.clear()

    def wait_loads():
        for load in loads[2:]:
            load.wait()

    steps = {
        "ring1": first_ring, "pass1": first_forward, "ring2": second_ring, "pass2": second_forward,
        "loads": wait_loads, "mult": multiply, "place": place, "z": z_step, "zend": z_end, "term": weight_term,
        "scatter": plane_scatter, "zsum": z_exchange, "gather": plane_gather, "core": core_gather,
        "out": weight_out, "rows": input_rows, "drain": drain,
    }
    for name, args in plan():
        steps[name](*args)
    drain(0)


def local(out_grad, state, features, weight, block_values, block_rows, block_cols, block_counts):
    values, rows, cols, count = block_values[0, 0], block_rows[0, 0], block_cols[0, 0], block_counts[0, 0]
    slot = jnp.arange(SLOTS, dtype=jnp.int32)
    key = jnp.where(slot < count, cols, 64)
    before = (key[None, :] < key[:, None]) | ((key[None, :] == key[:, None]) & (slot[None, :] < slot[:, None]))
    rank = jnp.sum(before.astype(jnp.int32), axis=1)
    first = jnp.sum(((key[None, :] == key[:, None]) & (slot[None, :] < slot[:, None])).astype(jnp.int32), axis=1) == 0
    device, b = rows // 4, rows % 4
    a0, a1 = device // 4, device % 4
    place = jnp.where(b < 2, a1 * 8 + a0 * 2 + b, 32 + a0 * 8 + a1 * 2 + b - 2)
    word = slot | (place << 8) | (first.astype(jnp.int32) << 16)
    packed = jnp.sum(jnp.where(rank[None, :] == slot[:, None], word[None, :], 0), axis=1)
    column = jnp.arange(64, dtype=jnp.int32)
    upto = jnp.sum((key[None, :] <= column[:, None]).astype(jnp.int32), axis=1)
    here = jnp.sum((key[None, :] == column[:, None]).astype(jnp.int32), axis=1)
    last = jnp.where(here > 0, upto - 1, SLOTS)

    anywhere = pl.BlockSpec(memory_space=pl.ANY)
    dma = pltpu.SemaphoreType.DMA
    grid = (512, 512)
    ig, wg = pl.pallas_call(
        kernel,
        out_shape=(jax.ShapeDtypeStruct(grid, BF), jax.ShapeDtypeStruct(grid, BF)),
        in_specs=[pl.BlockSpec(memory_space=pltpu.SMEM)] * 2 + [anywhere] * 5,
        out_specs=(pl.BlockSpec(memory_space=pltpu.VMEM), pl.BlockSpec(memory_space=pltpu.VMEM)),
        scratch_shapes=[pltpu.VMEM((64, size, B), BF) for _, size in CUTS]
        + [pltpu.VMEM(grid, BF)] * 4
        + [
            pltpu.VMEM((SLOTS, B, B), BF),
            pltpu.VMEM((SLOTS + 1, B, B), BF),
            pltpu.VMEM((B, B), F32),
            pltpu.VMEM((64, 512, B), BF),
            pltpu.VMEM((32, 512, B), BF),
            pltpu.VMEM((8, 4, 512, B), BF),
            pltpu.VMEM((8, 4, 512, B), BF),
            pltpu.VMEM((4, 512, B), BF),
            pltpu.VMEM((UNITS, B, 512), F32),
            pltpu.VMEM((UNITS, 64, 512), BF),
            pltpu.VMEM((UNITS, 64, 512), BF),
            pltpu.VMEM((UNITS, 16, 16, B), BF),
            pltpu.VMEM((UNITS, 15, 16, B), BF),
            pltpu.VMEM((UNITS, 8, 16, B), BF),
            pltpu.VMEM((UNITS, 2, 16, 16, B), BF),
            dma((5,)),
            dma((CHUNKS * 20,)),
            dma((CHUNKS * 20,)),
            dma((CHUNKS * 8,)),
            dma((CHUNKS * 8,)),
            dma((CHUNKS * 14,)),
            dma((CHUNKS * 14,)),
            dma((UNITS,)),
            dma((UNITS,)),
            dma((UNITS * 15,)),
            dma((UNITS * 15,)),
            dma((UNITS * 7,)),
            dma((UNITS * 7,)),
            dma((UNITS * 15,)),
            dma((UNITS * 15,)),
            dma((UNITS,)),
            dma((UNITS,)),
        ],
        compiler_params=pltpu.CompilerParams(
            collective_id=0, has_side_effects=True, vmem_limit_bytes=56 * 1024 * 1024
        ),
        name="graph_backward",
    )(packed, last, out_grad, state, features, weight, values)
    nodes = 512 * lax.axis_size("gr") * lax.axis_size("gc")
    return ig, wg.astype(F32) * nodes ** (-0.5)


def solution(mesh):
    in_specs = (
        P(("gr", "gc"), None),
        P(("gr", "gc"), None),
        P(("gc", "gr"), None),
        P(),
        P("gr", "gc", None, None, None),
        P("gr", "gc", None),
        P("gr", "gc", None),
        P("gr", "gc"),
    )
    out_specs = (P(("gc", "gr"), None), P())
    return jax.shard_map(local, mesh=mesh, in_specs=in_specs, out_specs=out_specs, check_vma=False)
```

time: 148 us -> 118 us (0.80)
  Pallas kernels: 139 us -> 109 us
    pallas_call x1, Pallas kernels: 139 us -> 109 us  [local(): pl.pallas_call(kernel, out_shape=(jax.ShapeDtypeStruct(grid, BF), jax.Sha...]
    unnamed x2 -> x1, local copies, waits for them, and re-layouts: 3.18 us -> 1.87 us
where the time goes in v2:
time: 118 us; the launch traced here: 117 us
  Pallas kernels  109 us (92%)
  other arithmetic  5.1 us (4%)
  local copies, waits for them, and re-layouts  1.87 us (2%)
  between operations  1.29 us (1%)
    pallas_call x1, Pallas kernels, local(): pl.pallas_call(kernel, out_shape=(jax.ShapeDtypeStruct(grid, BF), jax.Sha...  109 us

profile of v2, /device:TPU:1, one launch (start us, length us, event | category | flops | bytes accessed | tf_op | source)
XLA Modules:
  0.0 117.4 jit_solution(1760699719164987869)
XLA Ops:
  1.3 0.7 compare_select_fusion.2
  2.0 0.1 convert_reduce_fusion.2
  2.1 0.5 compare_select_fusion.last
  2.6 0.2 convert_reduce_fusion.1
  2.8 0.7 fusion.3
  3.5 0.7 select_reduce_fusion.packed
  4.2 109.2 %graph_backward.1 = (bf16[512,512]{1,0:T(8,128)(2,1)}, bf16[512,512]{1,0:T(8,128)(2,1)}) custom-call(s32[152]{0:T(256)} %select_reduce_fusion.packed, s32[64]{0:T(128)} %compare_select_fusion.last, bf16[512,512]{1,0:T(8,128)(2,1)} %og_h.1, bf16[512,512]{1,0:T(8,128)(2,1)} %pre_h.1, bf16[512,512]{1,0:T(8,128)(2,1)} %feat_h.1, bf16[512,512]{1,0:T(8,128)(2,1)} %w_h.1, ...), custom_call_target="tpu_custom_call" | custom-call | tf_op jit(solution)/shard_map/graph_backward/pallas_call | solution.py:393
  113.4 2.2 %convert_multiply_fusion = f32[512,512]{1,0:T(8,128)} fusion(bf16[512,512]{1,0:T(8,128)(2,1)} %get-tuple-element.5), kind=kLoop, calls=%fused_computation | loop fusion | flops 524288 | bytes 1572864 | tf_op jit(solution)/shard_map/mul | solution.py:440
  115.6 1.9 %copy.12 = bf16[512,512]{1,0:T(8,128)(2,1)} copy(bf16[512,512]{1,0:T(8,128)(2,1)} %get-tuple-element.12) | data formatting | bytes 1048576

commit v3 on v2

v3 whole, which is shorter than its diff:
```python
import functools

import jax
import jax.numpy as jnp
from jax import lax
from jax.experimental import pallas as pl
from jax.experimental.pallas import tpu as pltpu
from jax.sharding import PartitionSpec as P

MESH = pl.DeviceIdType.MESH
B = 128
SLOTS = 152
CUTS = ((0, 64), (64, 64), (128, 64), (192, 64), (256, 128), (384, 80), (464, 48))
CHUNKS = len(CUTS)
UNITS = 4
UNROLL = 19
BF = jnp.bfloat16
F32 = jnp.float32


GROUPS = ((4, 3, 5), (2, 6), (1, 7, 0))


def plan():
    tasks = {}

    def task(name, args, after=(), needs=(), sends=(), cost=0.1, rank=0.0):
        tasks[name, args] = (tuple(after), tuple(needs), tuple(sends), cost, rank)

    chip, core = 2.4, 0.9
    task("loads", (), cost=1.5, rank=-5)
    for k, (at, size) in enumerate(CUTS):
        unit = size / 2
        task("ring1", (k,), [("ring1", (k - 1,))] if k else [], (), [(("r1", k), "xy", unit, chip)], rank=-9)
        task("pass1", (k,), [], [("r1", k)], [(("f1", k), "xy", unit / 2, chip)], rank=-8)
        before = max(0, k - 1 - (size <= 64))
        gate = [("pass2", (before,))] if k > 1 else []
        task(
            "ring2", (k,), gate + ([("ring2", (k - 1,))] if k else []), [("f1", k)],
            [(("a", k), "xy", unit * 2, chip), (("b", k), "xy", unit * 2, chip)], rank=-7,
        )
        task("pass2", (k,), [], [("a", k)], [(("f2", k), "xy", unit * 2, chip)], rank=-8)
        load = 0.5 + size / 128
        follow = [("place", (k - 1, GROUPS[-1]))] if k else [("loads", ())]
        task("mult", (k, 0), follow, [("b", k), ("f2", k)], cost=load, rank=k)
        task("mult", (k, 1), [("mult", (k, 0))], cost=load, rank=k)
        for i, group in enumerate(GROUPS):
            task(
                "place", (k, group), [("place", (k, GROUPS[i - 1])) if i else ("mult", (k, 1))], (),
                [(("e", k, d), "core", size, core) for d in group], 0.08 * len(group), k - 0.5,
            )
        for chain in range(2):
            for t in range(4 - chain, 0, -1):
                needs = [("e", k, d) for d in sorted({t, 8 - t})]
                if t < 4 - chain:
                    needs.append(("z", k, chain, t + 1))
                task("z", (k, chain, t), (), needs, [(("z", k, chain, t), "z", size / 2, chip)], 0.2, -6 + k / 10)
        task("zend", (k,), (), [("e", k, 0), ("z", k, 0, 1), ("z", k, 1, 1)], cost=0.25, rank=-5 + k / 10)
    for u in range(UNITS):
        ends = [("zend", (k,)) for k, (at, _) in enumerate(CUTS) if at // B == u]
        task("term", (u,), ends, (), [(("t", u), "core", 64, core)], 0.7, u - 1)
        task("scatter", (u,), (), [("t", u)], [(("p", u), "xy", 32, 4.5)], 0.5, u - 1)
        behind = [("z", (CHUNKS - 1, 0, 1))] if u < UNITS - 1 else []
        task("zsum", (u,), behind, [("p", u)], [(("x", u), "z", 32, 4.5)], 0.4, u - 1)
        task("gather", (u,), (), [("x", u)], [(("q", u), "xy", 32, 4.5)], 0.5, u - 1)
        task("core", (u,), (), [("q", u)], [(("c", u), "core", 64, core)], 0.2, u - 1)
        task("out", (u,), (), [("c", u)], cost=0.4, rank=u + 1)
    for b in range(4):
        task("rows", (b,), [("zend", (CHUNKS - 1,)), ("scatter", (UNITS - 1,))], cost=0.6, rank=20)
    sums = [("z", (k, chain, 1)) for k in range(CHUNKS) for chain in range(2)]
    task("drain", (0,), [*sums, ("scatter", (UNITS - 1,))], cost=1.0, rank=30)
    task("drain", (1,), [("gather", (u,)) for u in range(UNITS)], cost=0.5, rank=30)

    now, free, come, done, order = 0.0, {"xy": 0.0, "z": 0.0, "core": 0.0}, {}, set(), []
    rate = {"xy": 48.0, "z": 48.0, "core": 600.0}
    while tasks:
        best = None
        for key, (after, needs, _, cost, rank) in tasks.items():
            if all(a in done for a in after) and all(n in come for n in needs):
                ready = max([now] + [come[n] for n in needs])
                score = (ready, rank)
                if best is None or score < best[0]:
                    best = (score, key)
        (now, _), key = best
        _, _, sends, cost, _ = tasks.pop(key)
        now += cost
        for message, link, kib, latency in sends:
            free[link] = max(free[link], now) + kib / rate[link]
            come[message] = free[link] + latency
        done.add(key)
        order.append(key)
    return order


def kernel(
    count, row_ids, col_ids, og_h, pre_h, feat_h, w_h, vals_h,
    ig_o, wg_o,
    g0, g1, g2, g3, g4, g5, g6, ids, table, lists, og, pre, feat, w, vals, prods, carry, part, sib, zs, zr, spread, term, tsend, trecv,
    psend, precv, zx, wg,
    local_sem, g_send, g_recv, e_send, e_recv, z_send, z_recv, t_send, t_recv, p_send, p_recv,
    x_send, x_recv, q_send, q_recv, c_send, c_recv,
):
    gathered = (g0, g1, g2, g3, g4, g5, g6)
    gr, gc = lax.axis_index("gr"), lax.axis_index("gc")
    scale = (512 * lax.axis_size("gr") * lax.axis_size("gc")) ** (-0.5)
    z, core = gr // 2, gr % 2
    x, y = gc // 4, gc % 4
    sibling = {"gr": z * 2 + (1 - core), "gc": gc}

    def z_peer(d):
        return {"gr": ((z + d) % 8) * 2 + core, "gc": gc}

    def plane_peer(d):
        return {"gr": gr, "gc": (gc + d) % 16}

    def x_peer(d):
        return {"gr": gr, "gc": ((x + d + 4) % 4) * 4 + y}

    def y_peer(d):
        return {"gr": gr, "gc": x * 4 + (y + d + 4) % 4}

    loads = [
        pltpu.make_async_copy(og_h, og, local_sem.at[0]),
        pltpu.make_async_copy(pre_h, pre, local_sem.at[1]),
        pltpu.make_async_copy(vals_h, vals, local_sem.at[2]),
        pltpu.make_async_copy(feat_h, feat, local_sem.at[3]),
        pltpu.make_async_copy(w_h, w, local_sem.at[4]),
    ]
    for load in loads:
        load.start()

    barrier = pltpu.get_barrier_semaphore()
    pl.semaphore_signal(barrier, inc=1, device_id=sibling, device_id_type=MESH)

    for device in (z_peer(1), z_peer(7), x_peer(1), x_peer(-1), y_peer(1), y_peer(-1)):
        pl.semaphore_signal(barrier, inc=1, device_id=device, device_id_type=MESH)

    ring = (x, y)
    cross = (y, x)
    near = (x_peer, y_peer)
    far = (y_peer, x_peer)

    def unit(h, p, q):
        return h * 32 + p * 8 + q * 2

    loads[0].wait()
    loads[1].wait()
    for k in range(UNITS):
        for b in range(4):
            rows, cols = pl.ds(b * B, B), pl.ds(k * B, B)
            block = og[rows, cols]
            block = jnp.where(pre[rows, cols].astype(F32) > 0, block.astype(F32), 0.0).T.astype(BF)
            h = b // 2
            for n, (at, size) in enumerate(CUTS):
                if at // B == k:
                    gathered[n][unit(h, cross[h], ring[h]) + b % 2] = block[at % B : at % B + size]
    prods[SLOTS] = jnp.zeros((B, B), BF)
    pl.semaphore_wait(barrier, 7)

    def send(src, dst, send_sem, recv_sem, device):
        pltpu.make_async_remote_copy(
            src_ref=src, dst_ref=dst, send_sem=send_sem, recv_sem=recv_sem, device_id=device, device_id_type=MESH
        ).start()

    def bytes_of(ref, sem):
        return pltpu.make_async_remote_copy(
            src_ref=ref, dst_ref=ref, send_sem=sem, recv_sem=sem, device_id=sibling, device_id_type=MESH
        )

    def arrived(ref, sem):
        bytes_of(ref, sem).wait_recv()

    def left(ref, sem):
        bytes_of(ref, sem).wait_send()

    def gather_copy(stage, k, h, d, at, size, device):
        where = gathered[k].at[pl.ds(at, size)]
        send(where, where, g_send.at[k], g_recv.at[k * 4 + min(stage, 3)], device)

    def gather_arrived(k, stage, blocks):
        arrived(gathered[k].at[pl.ds(0, blocks)], g_recv.at[k * 4 + stage])

    def first_ring(k):
        for h in range(2):
            for d in (1, -1):
                gather_copy(0, k, h, d, unit(h, cross[h], ring[h]), 2, near[h](d))

    def first_forward(k):
        gather_arrived(k, 0, 8)
        for h in range(2):
            for d in (1, -1):
                came = (ring[h] - d + 4) % 4
                gather_copy(1, k, h, d, unit(h, cross[h], came) + (0 if d == 1 else 1), 1, near[h](d))

    def second_ring(k):
        gather_arrived(k, 1, 4)
        for part_no in range(2):
            for h in range(2):
                for d in (1, -1):
                    which = part_no if d == 1 else 1 - part_no
                    gather_copy(2 + part_no, k, h, d, unit(h, cross[h], 0) + 4 * which, 4, far[h](d))

    def second_forward(k):
        gather_arrived(k, 2, 16)
        for h in range(2):
            for d in (1, -1):
                came = (cross[h] - d + 4) % 4
                gather_copy(4, k, h, d, unit(h, came, 0) + (0 if d == 1 else 4), 4, far[h](d))

    def multiply(k, half):
        at, size = CUTS[k]
        source = gathered[k]
        if half == 0:
            gather_arrived(k, 3, 32)

        def some(t, total):
            for u in range(UNROLL):
                s = (half * 4 + t) * UNROLL + u
                word = lists[0, s]
                term_now = jnp.dot(source[(word >> 8) & 255], vals[word & 255], preferred_element_type=F32)
                total = jnp.where((word >> 16) != 0, term_now, total + term_now)
                prods[s, pl.ds(0, size)] = total.astype(BF)
            return total

        begin = jnp.zeros((size, B), F32) if half == 0 else carry[pl.ds(0, size), :]
        total = lax.fori_loop(0, SLOTS // UNROLL // 2, some, begin)
        if half == 0:
            carry[pl.ds(0, size), :] = total

    def place(k, group):
        at, size = CUTS[k]
        for d in group:
            zp = (z + d) % 8

            def one(j, _):
                part[zp * 8 + j, pl.ds(at, size)] = prods[lists[1, zp * 8 + j], pl.ds(0, size)]
                return 0

            lax.fori_loop(0, 8, one, 0, unroll=True)
            n = k * len(GROUPS) + GROUPS.index(group)
            send(
                part.at[pl.ds(zp * 8 + (1 - core) * 4, 4), pl.ds(at, size)],
                sib.at[pl.ds(zp * 4, 4), pl.ds(at, size)],
                e_send.at[k], e_recv.at[n], sibling,
            )

    exchanged = set()

    def own(k, d, b):
        group = next(n for n, members in enumerate(GROUPS) if d in members)
        if (k, group) not in exchanged:
            exchanged.add((k, group))
            arrived(sib.at[pl.ds(0, 4 * len(GROUPS[group])), pl.ds(*CUTS[k])], e_recv.at[k * len(GROUPS) + group])
        zp = (z + d) % 8
        cut = pl.ds(*CUTS[k])
        return part[zp * 8 + core * 4 + b, cut].astype(F32) + sib[zp * 4 + b, cut].astype(F32)

    def z_sem(k, chain, t):
        return z_recv.at[k * 7 + (t + 2 if chain == 0 else t - 1)]

    def z_step(k, chain, t):
        cut = pl.ds(*CUTS[k])
        fresh = t == 4 - chain
        if not fresh:
            arrived(zr.at[0, :, cut], z_sem(k, chain, t + 1))
        for side in range(2):
            h = side if chain == 0 else 1 - side
            d = 8 - t if side == 0 else t
            n = side * 4 + t - 1
            for b in (2 * h, 2 * h + 1):
                value = own(k, d, b)
                if not fresh:
                    value = value + zr[n + 1, b, cut].astype(F32)
                zs[n, b, cut] = value.astype(BF)
            blocks = pl.ds(2 * h, 2)
            send(
                zs.at[n, blocks, cut], zr.at[n, blocks, cut],
                z_send.at[k], z_sem(k, chain, t), z_peer(7 if side == 0 else 1),
            )

    def z_end(k):
        cut = pl.ds(*CUTS[k])
        for chain in range(2):
            arrived(zr.at[0, :, cut], z_sem(k, chain, 1))
        for b in range(4):
            total = own(k, 0, b) + zr[0, b, cut].astype(F32) + zr[4, b, cut].astype(F32)
            spread[b, cut] = total.astype(BF)

    def weight_term(k):
        total = jnp.dot(spread[0, pl.ds(k * B, B)], feat[pl.ds(0, B), :], preferred_element_type=F32)
        for b in range(1, 4):
            rows = spread[b, pl.ds(k * B, B)]
            total = total + jnp.dot(rows, feat[pl.ds(b * B, B), :], preferred_element_type=F32)
        term[k] = total
        tsend[k] = term[k, pl.ds((1 - core) * 64, 64), :].astype(BF)
        send(tsend.at[k], trecv.at[k], t_send.at[k], t_recv.at[k], sibling)

    def plane_scatter(k):
        arrived(trecv.at[k], t_recv.at[k])
        for a in range(4):
            for b in range(4):
                lanes = pl.ds(b * B, B)
                mine = term[k, pl.ds(core * 64 + a * 16, 16), lanes]
                psend[k, a * 4 + b] = (mine + trecv[k, pl.ds(a * 16, 16), lanes].astype(F32)).astype(BF)
        for o in range(1, 16):
            to = plane_peer(o)
            send(psend.at[k, to["gc"]], precv.at[k, o - 1], p_send.at[k], p_recv.at[k], to)

    def z_exchange(k):
        arrived(precv.at[k], p_recv.at[k])
        total = psend[k, gc].astype(F32)
        for o in range(1, 16):
            total = total + precv[k, o - 1].astype(F32)
        zx[k, z] = total.astype(BF)
        for o in range(1, 8):
            send(zx.at[k, z], zx.at[k, z], x_send.at[k], x_recv.at[k], z_peer(o))

    def plane_gather(k):
        arrived(zx.at[k, pl.ds(0, 7)], x_recv.at[k])
        total = zx[k, 0].astype(F32)
        for a in range(1, 8):
            total = total + zx[k, a].astype(F32)
        wg[k, core, gc] = total.astype(BF)
        for o in range(1, 16):
            send(wg.at[k, core, gc], wg.at[k, core, gc], q_send.at[k], q_recv.at[k], plane_peer(o))

    def core_gather(k):
        arrived(wg.at[k, core, pl.ds(0, 15)], q_recv.at[k])
        send(wg.at[k, core], wg.at[k, core], c_send.at[k], c_recv.at[k], sibling)

    def weight_out(k):
        arrived(wg.at[k, core], c_recv.at[k])
        for b in range(4):
            rows = [wg[k, c, a * 4 + b] for c in range(2) for a in range(4)]
            whole = jnp.concatenate(rows, axis=0).astype(F32)
            wg_o[pl.ds(b * B, B), pl.ds(k * B, B)] = whole.T * scale

    def input_rows(b):
        total = lax.dot_general(spread[b].T, w[...], (((1,), (1,)), ((), ())), preferred_element_type=F32)
        ig_o[pl.ds(b * B, B), :] = total.astype(BF)

    def drain(stage):
        if stage == 0:
            for k in range(CHUNKS):
                cut = pl.ds(*CUTS[k])
                left(gathered[k].at[pl.ds(0, 60)], g_send.at[k])
                left(sib.at[:, cut], e_send.at[k])
                left(zs.at[pl.ds(0, 7), :, cut], z_send.at[k])
            return
        for u in range(UNITS):
            if stage == 1:
                left(tsend.at[u], t_send.at[u])
                left(precv.at[u], p_send.at[u])
                left(zx.at[u, pl.ds(0, 7)], x_send.at[u])
            else:
                left(precv.at[u], q_send.at[u])
                left(wg.at[u, core], c_send.at[u])

    def wait_loads():
        ids[...] = jnp.zeros((8, 256), jnp.int32)
        ids[0:1, 0:SLOTS] = row_ids[0]
        ids[1:2, 0:SLOTS] = col_ids[0]
        slot, row = lax.broadcasted_iota(jnp.int32, (1, 256), 1), ids[0:1, :]
        quarter, device = row & 3, row >> 2
        a0, a1 = device >> 2, device & 3
        where = jnp.where(quarter < 2, a1 * 8 + a0 * 2 + quarter, 32 + a0 * 8 + a1 * 2 + quarter - 2)
        key = jnp.where(slot < count[0, 0], ids[1:2, :], 64)
        across, down = (lax.broadcasted_iota(jnp.int32, (256, 256), n) for n in (1, 0))
        key_across = jnp.broadcast_to(key, (256, 256))
        key_down = key_across.T
        word_down = jnp.broadcast_to(slot | (where << 8), (256, 256)).T
        same = (key_across == key_down) & (across < down)
        less = (key_across < key_down) | same
        rank = jnp.sum(less.astype(jnp.int32), axis=1, keepdims=True)
        opens = jnp.sum(same.astype(jnp.int32), axis=1, keepdims=True) == 0
        word_down = word_down | (opens.astype(jnp.int32) << 16)
        upto = jnp.sum((key_down <= across).astype(jnp.int32), axis=0, keepdims=True)
        here = jnp.sum((key_down == across).astype(jnp.int32), axis=0, keepdims=True)
        table[...] = jnp.zeros((8, 256), jnp.int32)
        table[0:1, :] = jnp.sum(jnp.where(rank == across, word_down, 0), axis=0, keepdims=True)
        table[1:2, :] = jnp.where(here > 0, upto - 1, SLOTS)
        pltpu.sync_copy(table, lists)
        for load in loads[2:]:
            load.wait()

    steps = {
        "ring1": first_ring, "pass1": first_forward, "ring2": second_ring, "pass2": second_forward,
        "loads": wait_loads, "mult": multiply, "place": place, "z": z_step, "zend": z_end, "term": weight_term,
        "scatter": plane_scatter, "zsum": z_exchange, "gather": plane_gather, "core": core_gather,
        "out": weight_out, "rows": input_rows, "drain": drain,
    }
    for name, args in plan():
        steps[name](*args)
    drain(2)


def finish(ig, wg, ig_o, wg_o):
    ig_o[...] = ig[...]
    wg_o[...] = wg[...]


def local(out_grad, state, features, weight, block_values, block_rows, block_cols, block_counts):
    anywhere = pl.BlockSpec(memory_space=pl.ANY)
    dma = pltpu.SemaphoreType.DMA
    grid = (512, 512)
    ig, wg = pl.pallas_call(
        kernel,
        out_shape=(jax.ShapeDtypeStruct(grid, BF), jax.ShapeDtypeStruct(grid, F32)),
        in_specs=[pl.BlockSpec(memory_space=pltpu.SMEM)] + [pl.BlockSpec(memory_space=pltpu.VMEM)] * 2 + [anywhere] * 5,
        out_specs=(pl.BlockSpec(memory_space=pltpu.VMEM), pl.BlockSpec(memory_space=pltpu.VMEM)),
        scratch_shapes=[pltpu.VMEM((64, size, B), BF) for _, size in CUTS]
        + [pltpu.VMEM((8, 256), jnp.int32)] * 2
        + [pltpu.SMEM((8, 256), jnp.int32)]
        + [pltpu.VMEM(grid, BF)] * 4
        + [
            pltpu.VMEM((SLOTS, B, B), BF),
            pltpu.VMEM((SLOTS + 1, B, B), BF),
            pltpu.VMEM((B, B), F32),
            pltpu.VMEM((64, 512, B), BF),
            pltpu.VMEM((32, 512, B), BF),
            pltpu.VMEM((8, 4, 512, B), BF),
            pltpu.VMEM((8, 4, 512, B), BF),
            pltpu.VMEM((4, 512, B), BF),
            pltpu.VMEM((UNITS, B, 512), F32),
            pltpu.VMEM((UNITS, 64, 512), BF),
            pltpu.VMEM((UNITS, 64, 512), BF),
            pltpu.VMEM((UNITS, 16, 16, B), BF),
            pltpu.VMEM((UNITS, 15, 16, B), BF),
            pltpu.VMEM((UNITS, 8, 16, B), BF),
            pltpu.VMEM((UNITS, 2, 16, 16, B), BF),
            dma((5,)),
            dma((CHUNKS,)),
            dma((CHUNKS * 4,)),
            dma((CHUNKS,)),
            dma((CHUNKS * len(GROUPS),)),
            dma((CHUNKS,)),
            dma((CHUNKS * 7,)),
        ]
        + [dma((UNITS,))] * 10,
        compiler_params=pltpu.CompilerParams(
            collective_id=0, has_side_effects=True, vmem_limit_bytes=56 * 1024 * 1024
        ),
        name="graph_backward",
    )(block_counts, block_rows, block_cols, out_grad, state, features, weight, block_values[0, 0])
    return pl.pallas_call(
        finish,
        out_shape=(jax.ShapeDtypeStruct(grid, BF), jax.ShapeDtypeStruct(grid, F32)),
        name="finish",
    )(ig, wg)


def solution(mesh):
    in_specs = (
        P(("gr", "gc"), None),
        P(("gr", "gc"), None),
        P(("gc", "gr"), None),
        P(),
        P("gr", "gc", None, None, None),
        P("gr", "gc", None),
        P("gr", "gc", None),
        P("gr", "gc"),
    )
    out_specs = (P(("gc", "gr"), None), P())
    return jax.shard_map(local, mesh=mesh, in_specs=in_specs, out_specs=out_specs, check_vma=False)
```

time: 118 us -> 105 us (0.89)
  other arithmetic: 5.1 us -> 0 us
  Pallas kernels: 109 us -> 104 us
  local copies, waits for them, and re-layouts: 1.87 us -> 0 us
    pallas_call x1, Pallas kernels: 109 us -> 101 us  [local(): pl.pallas_call(kernel, out_shape=(jax.ShapeDtypeStruct(grid, BF), jax.Sha...]
    pallas_call x0 -> x1, Pallas kernels: none -> 2.57 us  [local(): pl.pallas_call(finish, out_shape=(jax.ShapeDtypeStruct(grid, BF), jax.Sha...]
    mul x1 -> x0, other arithmetic: 2.16 us -> none  [local(): return (ig, wg.astype(F32) * nodes ** (-0.5))]
    unnamed x1 -> x0, local copies, waits for them, and re-layouts: 1.87 us -> none
    select_n x2 -> x0, other arithmetic: 1.2 us -> none  [the longest x1 0.68 us: local(): key = jnp.where(slot < count, cols, 64)]
where the time goes in v3:
time: 105 us
  Pallas kernels  104 us (99%)
  between operations  1.29 us (1%)
    pallas_call x1, Pallas kernels, local(): pl.pallas_call(kernel, out_shape=(jax.ShapeDtypeStruct(grid, BF), jax.Sha...  101 us
    pallas_call x1, Pallas kernels, local(): pl.pallas_call(finish, out_shape=(jax.ShapeDtypeStruct(grid, BF), jax.Sha...  2.57 us

profile of v3, /device:TPU:1, one launch (start us, length us, event | category | flops | bytes accessed | tf_op | source)
XLA Modules:
  0.0 104.9 jit_solution(13966194914486056327)
XLA Ops:
  1.3 101.0 %graph_backward.1 = (bf16[512,512]{1,0:T(8,128)(2,1)}, f32[512,512]{1,0:T(8,128)}) custom-call(s32[1,1]{1,0:T(1,128)S(6)} %copy.10.count, s32[1,1,152]{2,1,0:T(1,128)} %row_ids.1, s32[1,1,152]{2,1,0:T(1,128)} %col_ids.1, bf16[512,512]{1,0:T(8,128)(2,1)} %og_h.1, bf16[512,512]{1,0:T(8,128)(2,1)} %pre_h.1, bf16[512,512]{1,0:T(8,128)(2,1)} %feat_h.1, ...), custom_call_target="tpu_custom_call" | custom-call | tf_op jit(solution)/shard_map/graph_backward/pallas_call | solution.py:406
  102.3 2.6 %finish.1 = (bf16[512,512]{1,0:T(8,128)(2,1)}, f32[512,512]{1,0:T(8,128)}) custom-call(bf16[512,512]{1,0:T(8,128)(2,1)} %get-tuple-element.4.ig, f32[512,512]{1,0:T(8,128)} %get-tuple-element.5.wg), custom_call_target="tpu_custom_call" | custom-call | tf_op jit(solution)/shard_map/finish/pallas_call | solution.py:445

commit v4 on v3

--- a/solution.py
+++ b/solution.py
@@ -10,10 +10,10 @@
 MESH = pl.DeviceIdType.MESH
 B = 128
 SLOTS = 152
-CUTS = ((0, 64), (64, 64), (128, 64), (192, 64), (256, 128), (384, 80), (464, 48))
+CUTS = ((0, 64), (64, 64), (128, 64), (192, 64), (256, 64), (320, 64), (384, 128))
 CHUNKS = len(CUTS)
 UNITS = 4
-UNROLL = 19
+UNROLL = 38
 BF = jnp.bfloat16
 F32 = jnp.float32
 
@@ -28,7 +28,7 @@
         tasks[name, args] = (tuple(after), tuple(needs), tuple(sends), cost, rank)
 
     chip, core = 2.4, 0.9
-    task("loads", (), cost=1.5, rank=-5)
+    task("loads", (), cost=1.2, rank=-5)
     for k, (at, size) in enumerate(CUTS):
         unit = size / 2
         task("ring1", (k,), [("ring1", (k - 1,))] if k else [], (), [(("r1", k), "xy", unit, chip)], rank=-9)
@@ -40,7 +40,7 @@
             [(("a", k), "xy", unit * 2, chip), (("b", k), "xy", unit * 2, chip)], rank=-7,
         )
         task("pass2", (k,), [], [("a", k)], [(("f2", k), "xy", unit * 2, chip)], rank=-8)
-        load = 0.5 + size / 128
+        load = 0.95
         follow = [("place", (k - 1, GROUPS[-1]))] if k else [("loads", ())]
         task("mult", (k, 0), follow, [("b", k), ("f2", k)], cost=load, rank=k)
         task("mult", (k, 1), [("mult", (k, 0))], cost=load, rank=k)
@@ -215,7 +215,7 @@
 
         def some(t, total):
             for u in range(UNROLL):
-                s = (half * 4 + t) * UNROLL + u
+                s = (half * 2 + t) * UNROLL + u
                 word = lists[0, s]
                 term_now = jnp.dot(source[(word >> 8) & 255], vals[word & 255], preferred_element_type=F32)
                 total = jnp.where((word >> 16) != 0, term_now, total + term_now)
@@ -394,9 +394,12 @@
     drain(2)
 
 
-def finish(ig, wg, ig_o, wg_o):
-    ig_o[...] = ig[...]
-    wg_o[...] = wg[...]
+def finish(ig, wg, ig_o, wg_o, sems):
+    copies = [pltpu.make_async_copy(ig, ig_o, sems.at[0]), pltpu.make_async_copy(wg, wg_o, sems.at[1])]
+    for copy in copies:
+        copy.start()
+    for copy in copies:
+        copy.wait()
 
 
 def local(out_grad, state, features, weight, block_values, block_rows, block_cols, block_counts):
@@ -405,7 +408,7 @@
     grid = (512, 512)
     ig, wg = pl.pallas_call(
         kernel,
-        out_shape=(jax.ShapeDtypeStruct(grid, BF), jax.ShapeDtypeStruct(grid, F32)),
+        out_shape=(pltpu.VMEM(grid, BF), pltpu.VMEM(grid, F32)),
         in_specs=[pl.BlockSpec(memory_space=pltpu.SMEM)] + [pl.BlockSpec(memory_space=pltpu.VMEM)] * 2 + [anywhere] * 5,
         out_specs=(pl.BlockSpec(memory_space=pltpu.VMEM), pl.BlockSpec(memory_space=pltpu.VMEM)),
         scratch_shapes=[pltpu.VMEM((64, size, B), BF) for _, size in CUTS]
@@ -445,8 +448,11 @@
     return pl.pallas_call(
         finish,
         out_shape=(jax.ShapeDtypeStruct(grid, BF), jax.ShapeDtypeStruct(grid, F32)),
+        in_specs=[pl.BlockSpec(memory_space=pltpu.VMEM)] * 2,
+        out_specs=(anywhere, anywhere),
+        scratch_shapes=[pltpu.SemaphoreType.DMA((2,))],
         name="finish",
-    )(ig, wg)
+    )(pltpu.with_memory_space_constraint(ig, pltpu.VMEM), pltpu.with_memory_space_constraint(wg, pltpu.VMEM))
 
 
 def solution(mesh):

time: 105 us -> 100 us (0.952)
  Pallas kernels: 104 us -> 98.6 us
    pallas_call x1, Pallas kernels: 101 us -> 97.4 us  [local(): pl.pallas_call(kernel, out_shape=(pltpu.VMEM(grid, BF), pltpu.VMEM(grid,...]
    pallas_call x1, Pallas kernels: 2.57 us -> 1.16 us  [local(): pl.pallas_call(finish, out_shape=(jax.ShapeDtypeStruct(grid, BF), jax.Sha...]
where the time goes in v4:
time: 100 us
  Pallas kernels  98.6 us (99%)
  between operations  1.45 us (1%)
    pallas_call x1, Pallas kernels, local(): pl.pallas_call(kernel, out_shape=(pltpu.VMEM(grid, BF), pltpu.VMEM(grid,...  97.4 us

profile of v4, /device:TPU:1, one launch (start us, length us, event | category | flops | bytes accessed | tf_op | source)
XLA Modules:
  0.0 100.0 jit_solution(17544390794560343316)
XLA Ops:
  1.3 97.4 %graph_backward.1 = (bf16[512,512]{1,0:T(8,128)(2,1)S(1)}, f32[512,512]{1,0:T(8,128)S(1)}) custom-call(s32[1,1]{1,0:T(1,128)S(6)} %copy.10.count, s32[1,1,152]{2,1,0:T(1,128)} %row_ids.1, s32[1,1,152]{2,1,0:T(1,128)} %col_ids.1, bf16[512,512]{1,0:T(8,128)(2,1)} %og_h.1, bf16[512,512]{1,0:T(8,128)(2,1)} %pre_h.1, bf16[512,512]{1,0:T(8,128)(2,1)} %feat_h.1, ...), custom_call_target="tpu_custom_call" | custom-call | tf_op jit(solution)/shard_map/graph_backward/pallas_call | solution.py:409
  98.7 1.2 %finish.1 = (bf16[512,512]{1,0:T(8,128)(2,1)}, f32[512,512]{1,0:T(8,128)}) custom-call(bf16[512,512]{1,0:T(8,128)(2,1)S(1)} %get-tuple-element.4.ig, f32[512,512]{1,0:T(8,128)S(1)} %get-tuple-element.5.wg), custom_call_target="tpu_custom_call" | custom-call | tf_op jit(solution)/shard_map/finish/pallas_call | solution.py:448

commit v5 on v4

--- a/solution.py
+++ b/solution.py
@@ -13,7 +13,7 @@
 CUTS = ((0, 64), (64, 64), (128, 64), (192, 64), (256, 64), (320, 64), (384, 128))
 CHUNKS = len(CUTS)
 UNITS = 4
-UNROLL = 38
+UNROLL = 76
 BF = jnp.bfloat16
 F32 = jnp.float32
 
@@ -119,14 +119,19 @@
     def y_peer(d):
         return {"gr": gr, "gc": x * 4 + (y + d + 4) % 4}
 
+    strips = []
+    for k in range(UNITS):
+        lanes = pl.ds(k * B, B)
+        strips.append([
+            pltpu.make_async_copy(og_h.at[:, lanes], og.at[:, lanes], local_sem.at[2 * k]),
+            pltpu.make_async_copy(pre_h.at[:, lanes], pre.at[:, lanes], local_sem.at[2 * k + 1]),
+        ])
     loads = [
-        pltpu.make_async_copy(og_h, og, local_sem.at[0]),
-        pltpu.make_async_copy(pre_h, pre, local_sem.at[1]),
-        pltpu.make_async_copy(vals_h, vals, local_sem.at[2]),
-        pltpu.make_async_copy(feat_h, feat, local_sem.at[3]),
-        pltpu.make_async_copy(w_h, w, local_sem.at[4]),
+        pltpu.make_async_copy(vals_h, vals, local_sem.at[8]),
+        pltpu.make_async_copy(feat_h, feat, local_sem.at[9]),
+        pltpu.make_async_copy(w_h, w, local_sem.at[10]),
     ]
-    for load in loads:
+    for load in [*strips[0], *strips[1], *strips[2], *strips[3], *loads]:
         load.start()
 
     barrier = pltpu.get_barrier_semaphore()
@@ -143,9 +148,9 @@
     def unit(h, p, q):
         return h * 32 + p * 8 + q * 2
 
-    loads[0].wait()
-    loads[1].wait()
-    for k in range(UNITS):
+    def mask(k):
+        for load in strips[k]:
+            load.wait()
         for b in range(4):
             rows, cols = pl.ds(b * B, B), pl.ds(k * B, B)
             block = og[rows, cols]
@@ -154,6 +159,8 @@
             for n, (at, size) in enumerate(CUTS):
                 if at // B == k:
                     gathered[n][unit(h, cross[h], ring[h]) + b % 2] = block[at % B : at % B + size]
+
+    mask(0)
     prods[SLOTS] = jnp.zeros((B, B), BF)
     pl.semaphore_wait(barrier, 7)
 
@@ -175,12 +182,15 @@
 
     def gather_copy(stage, k, h, d, at, size, device):
         where = gathered[k].at[pl.ds(at, size)]
-        send(where, where, g_send.at[k], g_recv.at[k * 4 + min(stage, 3)], device)
+        send(where, where, g_send.at[0], g_recv.at[k * 4 + min(stage, 3)], device)
 
     def gather_arrived(k, stage, blocks):
         arrived(gathered[k].at[pl.ds(0, blocks)], g_recv.at[k * 4 + stage])
 
     def first_ring(k):
+        at = CUTS[k][0]
+        if at and at % B == 0:
+            mask(at // B)
         for h in range(2):
             for d in (1, -1):
                 gather_copy(0, k, h, d, unit(h, cross[h], ring[h]), 2, near[h](d))
@@ -215,7 +225,7 @@
 
         def some(t, total):
             for u in range(UNROLL):
-                s = (half * 2 + t) * UNROLL + u
+                s = (half + t) * UNROLL + u
                 word = lists[0, s]
                 term_now = jnp.dot(source[(word >> 8) & 255], vals[word & 255], preferred_element_type=F32)
                 total = jnp.where((word >> 16) != 0, term_now, total + term_now)
@@ -241,7 +251,7 @@
             send(
                 part.at[pl.ds(zp * 8 + (1 - core) * 4, 4), pl.ds(at, size)],
                 sib.at[pl.ds(zp * 4, 4), pl.ds(at, size)],
-                e_send.at[k], e_recv.at[n], sibling,
+                e_send.at[0], e_recv.at[n], sibling,
             )
 
     exchanged = set()
@@ -275,7 +285,7 @@
             blocks = pl.ds(2 * h, 2)
             send(
                 zs.at[n, blocks, cut], zr.at[n, blocks, cut],
-                z_send.at[k], z_sem(k, chain, t), z_peer(7 if side == 0 else 1),
+                z_send.at[0], z_sem(k, chain, t), z_peer(7 if side == 0 else 1),
             )
 
     def z_end(k):
@@ -293,7 +303,7 @@
             total = total + jnp.dot(rows, feat[pl.ds(b * B, B), :], preferred_element_type=F32)
         term[k] = total
         tsend[k] = term[k, pl.ds((1 - core) * 64, 64), :].astype(BF)
-        send(tsend.at[k], trecv.at[k], t_send.at[k], t_recv.at[k], sibling)
+        send(tsend.at[k], trecv.at[k], t_send.at[0], t_recv.at[k], sibling)
 
     def plane_scatter(k):
         arrived(trecv.at[k], t_recv.at[k])
@@ -304,7 +314,7 @@
                 psend[k, a * 4 + b] = (mine + trecv[k, pl.ds(a * 16, 16), lanes].astype(F32)).astype(BF)
         for o in range(1, 16):
             to = plane_peer(o)
-            send(psend.at[k, to["gc"]], precv.at[k, o - 1], p_send.at[k], p_recv.at[k], to)
+            send(psend.at[k, to["gc"]], precv.at[k, o - 1], p_send.at[0], p_recv.at[k], to)
 
     def z_exchange(k):
         arrived(precv.at[k], p_recv.at[k])
@@ -313,7 +323,7 @@
             total = total + precv[k, o - 1].astype(F32)
         zx[k, z] = total.astype(BF)
         for o in range(1, 8):
-            send(zx.at[k, z], zx.at[k, z], x_send.at[k], x_recv.at[k], z_peer(o))
+            send(zx.at[k, z], zx.at[k, z], x_send.at[0], x_recv.at[k], z_peer(o))
 
     def plane_gather(k):
         arrived(zx.at[k, pl.ds(0, 7)], x_recv.at[k])
@@ -322,11 +332,11 @@
             total = total + zx[k, a].astype(F32)
         wg[k, core, gc] = total.astype(BF)
         for o in range(1, 16):
-            send(wg.at[k, core, gc], wg.at[k, core, gc], q_send.at[k], q_recv.at[k], plane_peer(o))
+            send(wg.at[k, core, gc], wg.at[k, core, gc], q_send.at[0], q_recv.at[k], plane_peer(o))
 
     def core_gather(k):
         arrived(wg.at[k, core, pl.ds(0, 15)], q_recv.at[k])
-        send(wg.at[k, core], wg.at[k, core], c_send.at[k], c_recv.at[k], sibling)
+        send(wg.at[k, core], wg.at[k, core], c_send.at[0], c_recv.at[k], sibling)
 
     def weight_out(k):
         arrived(wg.at[k, core], c_recv.at[k])
@@ -341,20 +351,16 @@
 
     def drain(stage):
         if stage == 0:
-            for k in range(CHUNKS):
-                cut = pl.ds(*CUTS[k])
-                left(gathered[k].at[pl.ds(0, 60)], g_send.at[k])
-                left(sib.at[:, cut], e_send.at[k])
-                left(zs.at[pl.ds(0, 7), :, cut], z_send.at[k])
-            return
-        for u in range(UNITS):
-            if stage == 1:
-                left(tsend.at[u], t_send.at[u])
-                left(precv.at[u], p_send.at[u])
-                left(zx.at[u, pl.ds(0, 7)], x_send.at[u])
-            else:
-                left(precv.at[u], q_send.at[u])
-                left(wg.at[u, core], c_send.at[u])
+            left(part.at[pl.ds(0, 60)], g_send.at[0])
+            left(sib, e_send.at[0])
+            left(zs.at[pl.ds(0, 7)], z_send.at[0])
+        elif stage == 1:
+            left(tsend, t_send.at[0])
+            left(precv, p_send.at[0])
+            left(zx.at[:, pl.ds(0, 7)], x_send.at[0])
+        else:
+            left(precv, q_send.at[0])
+            left(wg.at[:, core], c_send.at[0])
 
     def wait_loads():
         ids[...] = jnp.zeros((8, 256), jnp.int32)
@@ -380,7 +386,7 @@
         table[0:1, :] = jnp.sum(jnp.where(rank == across, word_down, 0), axis=0, keepdims=True)
         table[1:2, :] = jnp.where(here > 0, upto - 1, SLOTS)
         pltpu.sync_copy(table, lists)
-        for load in loads[2:]:
+        for load in loads:
             load.wait()
 
     steps = {
@@ -431,15 +437,15 @@
             pltpu.VMEM((UNITS, 15, 16, B), BF),
             pltpu.VMEM((UNITS, 8, 16, B), BF),
             pltpu.VMEM((UNITS, 2, 16, 16, B), BF),
-            dma((5,)),
-            dma((CHUNKS,)),
+            dma((11,)),
+            dma((1,)),
             dma((CHUNKS * 4,)),
-            dma((CHUNKS,)),
+            dma((1,)),
             dma((CHUNKS * len(GROUPS),)),
-            dma((CHUNKS,)),
+            dma((1,)),
             dma((CHUNKS * 7,)),
         ]
-        + [dma((UNITS,))] * 10,
+        + [dma((1,)), dma((UNITS,))] * 5,
         compiler_params=pltpu.CompilerParams(
             collective_id=0, has_side_effects=True, vmem_limit_bytes=56 * 1024 * 1024
         ),

time: 100 us -> 99.4 us (level)
  no operation moved by 1% of the time
where the time goes in v5:
time: 99.4 us; the launch traced here: 99.3 us
  Pallas kernels  97.8 us (98%)
  between operations  1.45 us (1%)
    pallas_call x1, Pallas kernels, local(): pl.pallas_call(kernel, out_shape=(pltpu.VMEM(grid, BF), pltpu.VMEM(grid,...  96.6 us

profile of v5, /device:TPU:1, one launch (start us, length us, event | category | flops | bytes accessed | tf_op | source)
XLA Modules:
  0.0 99.3 jit_solution(370738722381654745)
XLA Ops:
  1.3 96.6 %graph_backward.1 = (bf16[512,512]{1,0:T(8,128)(2,1)S(1)}, f32[512,512]{1,0:T(8,128)S(1)}) custom-call(s32[1,1]{1,0:T(1,128)S(6)} %copy.10.count, s32[1,1,152]{2,1,0:T(1,128)} %row_ids.1, s32[1,1,152]{2,1,0:T(1,128)} %col_ids.1, bf16[512,512]{1,0:T(8,128)(2,1)} %og_h.1, bf16[512,512]{1,0:T(8,128)(2,1)} %pre_h.1, bf16[512,512]{1,0:T(8,128)(2,1)} %feat_h.1, ...), custom_call_target="tpu_custom_call" | custom-call | tf_op jit(solution)/shard_map/graph_backward/pallas_call | solution.py:415
  97.9 1.2 %finish.1 = (bf16[512,512]{1,0:T(8,128)(2,1)}, f32[512,512]{1,0:T(8,128)}) custom-call(bf16[512,512]{1,0:T(8,128)(2,1)S(1)} %get-tuple-element.4.ig, f32[512,512]{1,0:T(8,128)S(1)} %get-tuple-element.5.wg), custom_call_target="tpu_custom_call" | custom-call | tf_op jit(solution)/shard_map/finish/pallas_call | solution.py:454

commit v6 on v5

--- a/solution.py
+++ b/solution.py
@@ -27,8 +27,8 @@
     def task(name, args, after=(), needs=(), sends=(), cost=0.1, rank=0.0):
         tasks[name, args] = (tuple(after), tuple(needs), tuple(sends), cost, rank)
 
-    chip, core = 2.4, 0.9
-    task("loads", (), cost=1.2, rank=-5)
+    chip, core = 2.2, 0.9
+    task("loads", (), cost=1.2, rank=-7.5)
     for k, (at, size) in enumerate(CUTS):
         unit = size / 2
         task("ring1", (k,), [("ring1", (k - 1,))] if k else [], (), [(("r1", k), "xy", unit, chip)], rank=-9)

time: 99.4 us -> 100 us (level)
  no operation moved by 1% of the time
where the time goes in v6:
time: 100 us
  Pallas kernels  98.6 us (99%)
  between operations  1.45 us (1%)
    pallas_call x1, Pallas kernels, local(): pl.pallas_call(kernel, out_shape=(pltpu.VMEM(grid, BF), pltpu.VMEM(grid,...  97.4 us

profile of v6, /device:TPU:1, one launch (start us, length us, event | category | flops | bytes accessed | tf_op | source)
XLA Modules:
  0.0 100.0 jit_solution(356252573519965827)
XLA Ops:
  1.3 97.4 %graph_backward.1 = (bf16[512,512]{1,0:T(8,128)(2,1)S(1)}, f32[512,512]{1,0:T(8,128)S(1)}) custom-call(s32[1,1]{1,0:T(1,128)S(6)} %copy.10.count, s32[1,1,152]{2,1,0:T(1,128)} %row_ids.1, s32[1,1,152]{2,1,0:T(1,128)} %col_ids.1, bf16[512,512]{1,0:T(8,128)(2,1)} %og_h.1, bf16[512,512]{1,0:T(8,128)(2,1)} %pre_h.1, bf16[512,512]{1,0:T(8,128)(2,1)} %feat_h.1, ...), custom_call_target="tpu_custom_call" | custom-call | tf_op jit(solution)/shard_map/graph_backward/pallas_call | solution.py:415
  98.7 1.2 %finish.1 = (bf16[512,512]{1,0:T(8,128)(2,1)}, f32[512,512]{1,0:T(8,128)}) custom-call(bf16[512,512]{1,0:T(8,128)(2,1)S(1)} %get-tuple-element.4.ig, f32[512,512]{1,0:T(8,128)S(1)} %get-tuple-element.5.wg), custom_call_target="tpu_custom_call" | custom-call | tf_op jit(solution)/shard_map/finish/pallas_call | solution.py:454
